TPU v7x, 32 devices: a whole 2x2x4 slice. The times are simulated.
32 devices in a mesh: dp: 16 (over z, y, core), mp: 2 (over x).
Axes of the slice: x: 2, y: 2, z: 4, core: 2. Of those that a mesh axis runs over, the one named last changes fastest.
Arguments:
- inputs: bfloat16 [32, 512, 768], P('dp', 'mp'), may hold values from -6 to 6
- pad_counts: int32 [32], P('dp'), may hold values from 0 to 32, as said below
- gainmix_one: bfloat16 [768], replicated, may hold values from 0.099609375 to 1.8984375
- shiftmix_one: bfloat16 [768], replicated, may hold values from -4 to 4
- upweight_one: bfloat16 [768, 3072], P(None, 'mp'), may hold values from -0.21875 to 0.21875
- upbias_one: bfloat16 [3072], P('mp'), may hold values from -6 to 6
- downweight_one: bfloat16 [3072, 768], P('mp'), may hold values from -0.109375 to 0.109375
- downbias_one: bfloat16 [768], replicated, may hold values from -6 to 6
- gainout_one: bfloat16 [768], replicated, may hold values from 0.099609375 to 1.8984375
- shiftout_one: bfloat16 [768], replicated, may hold values from -4 to 4
- gainmix_two: bfloat16 [768], replicated, may hold values from 0.099609375 to 1.8984375
- shiftmix_two: bfloat16 [768], replicated, may hold values from -4 to 4
- upweight_two: bfloat16 [768, 3072], P(None, 'mp'), may hold values from -0.21875 to 0.21875
- upbias_two: bfloat16 [3072], P('mp'), may hold values from -6 to 6
- downweight_two: bfloat16 [3072, 768], P('mp'), may hold values from -0.109375 to 0.109375
- downbias_two: bfloat16 [768], replicated, may hold values from -6 to 6
- gainout_two: bfloat16 [768], replicated, may hold values from 0.099609375 to 1.8984375
- shiftout_two: bfloat16 [768], replicated, may hold values from -4 to 4
- cotangent: bfloat16 [32, 512, 768], P('dp', 'mp'), may hold values from -6 to 6
Outputs:
- outputs: bfloat16 [32, 512, 768], P('dp', 'mp')
- input_grad: float32 [32, 512, 768], P('dp', 'mp')
- gradgainmix_one: float32 [768], replicated
- gradshiftmix_one: float32 [768], replicated
- gradupweight_one: float32 [768, 3072], P(None, 'mp')
- gradupbias_one: float32 [3072], P('mp')
- graddownweight_one: float32 [3072, 768], P('mp')
- graddownbias_one: float32 [768], replicated
- gradgainout_one: float32 [768], replicated
- gradshiftout_one: float32 [768], replicated
- gradgainmix_two: float32 [768], replicated
- gradshiftmix_two: float32 [768], replicated
- gradupweight_two: float32 [768, 3072], P(None, 'mp')
- gradupbias_two: float32 [3072], P('mp')
- graddownweight_two: float32 [3072, 768], P('mp')
- graddownbias_two: float32 [768], replicated
- gradgainout_two: float32 [768], replicated
- gradshiftout_two: float32 [768], replicated
Inputs may be any that keep to these rules, and one draw needn't show every extreme that they name: `pad_counts`: some row has exactly 32 pad slots and some row has none.
All inputs are finite; a program needn't handle non-finite values.
Results may differ from a plain program's by a relative error of at most 0.023.
Values may be sent and summed in bfloat16 or wider, within the bound.
No kernel may reach another device: no remote copies, remote signals or barrier semaphores. Data moves between devices by JAX's collectives and lax.ppermute only.
A program may use at most 128 MiB of HBM per device.

v0:
```python
import math

import jax
import jax.numpy as jnp
from jax import lax
from jax.sharding import PartitionSpec as P

norm_eps = 1e-05


def fourier_table(points):
    indices = jnp.arange(points, dtype=jnp.int32)
    phases = indices[:, None] * indices[None, :] % points
    angles = phases.astype(jnp.float32) * (2.0 * math.pi / points)
    factor = points ** (-0.5)
    return (jnp.cos(angles) * factor, jnp.sin(angles) * factor)


def layer_norm(activity, gain_vec, shift_vec):
    center = jnp.mean(activity, axis=-1, keepdims=True)
    centered = activity - center
    spread = jnp.mean(centered * centered, axis=-1, keepdims=True)
    return centered * lax.rsqrt(spread + norm_eps) * gain_vec + shift_vec


def smooth_gate(activity):
    return jax.nn.gelu(activity, approximate=True)


def gate_backward(preact, hidden_grad):
    gate_value, gate_pull = jax.vjp(smooth_gate, preact)
    return gate_pull(hidden_grad)[0].astype(jnp.bfloat16)


def spectra_forward(spectra, own_pair):

    def add_block(totals, row_piece, offset):
        return jnp.einsum("tcn,rncd->rtd", own_pair, row_piece, preferred_element_type=jnp.float32)

    initial = jnp.zeros((spectra.shape[0], spectra.shape[1], spectra.shape[3]), jnp.float32)
    return add_block(initial, lax.all_gather(spectra, "mp", axis=1, tiled=True), jnp.int32(0))


def spectra_backward(mixed_cot, own_pair):

    def add_block(totals, row_piece, offset):
        return jnp.einsum("tcn,rnd->rtcd", own_pair, row_piece, preferred_element_type=jnp.float32)

    initial = jnp.zeros(
        (mixed_cot.shape[0], mixed_cot.shape[1], 2, mixed_cot.shape[2]), jnp.float32
    )
    return add_block(
        initial, lax.all_gather(mixed_cot, "mp", axis=1, tiled=True), jnp.int32(0)
    ).astype(jnp.bfloat16)


def feed_forward(normed_low, up_weight, up_bias, down_weight, down_bias):
    gathered = lax.all_gather(normed_low, "mp", axis=1, tiled=True)
    preact = (
        jnp.einsum("rtd,df->rtf", gathered, up_weight, preferred_element_type=jnp.float32) + up_bias
    )
    hidden = smooth_gate(preact).astype(jnp.bfloat16)
    partial_sum = jnp.einsum("rtf,fd->rtd", hidden, down_weight, preferred_element_type=jnp.float32)
    branch = (
        lax.psum_scatter(
            partial_sum.astype(jnp.bfloat16), "mp", scatter_dimension=1, tiled=True
        ).astype(jnp.float32)
        + down_bias
    )
    return (branch, (gathered, preact, hidden, up_weight, down_weight))


def feed_backward(branch_cot, kept):
    gathered, preact, hidden, up_weight, down_weight = kept
    cot_rows = lax.all_gather(branch_cot, "mp", axis=1, tiled=True)
    down_grad = jnp.einsum("rtf,rtd->fd", hidden, cot_rows, preferred_element_type=jnp.float32)
    hidden_grad = jnp.einsum(
        "rtd,fd->rtf", cot_rows, down_weight, preferred_element_type=jnp.float32
    )
    preact_cot = gate_backward(preact, hidden_grad)
    up_grad = jnp.einsum("rtd,rtf->df", gathered, preact_cot, preferred_element_type=jnp.float32)
    upbias_grad = jnp.sum(preact_cot, axis=(0, 1), dtype=jnp.float32)
    partial_grad = jnp.einsum(
        "rtf,df->rtd", preact_cot, up_weight, preferred_element_type=jnp.float32
    )
    normed_grad = lax.psum_scatter(
        partial_grad.astype(jnp.bfloat16), "mp", scatter_dimension=1, tiled=True
    ).astype(jnp.float32)
    return (normed_grad, (up_grad, upbias_grad, down_grad))


def layer_forward(layer_in, live_mask, params, tables):
    gain_mix, shift_mix, up_weight, up_bias, down_weight, down_bias, gain_out, shift_out = params
    own_pair, pair_full, wide_table = tables
    masked = layer_in * live_mask
    spectra = jnp.einsum(
        "rtd,dk->rtk", masked.astype(jnp.bfloat16), wide_table, preferred_element_type=jnp.float32
    ).astype(jnp.bfloat16)
    spectra = spectra.reshape(spectra.shape[0], spectra.shape[1], 2, wide_table.shape[0])
    mixed = spectra_forward(spectra, own_pair)
    summed = masked + mixed
    normed = layer_norm(summed, gain_mix.astype(jnp.float32), shift_mix.astype(jnp.float32))
    branch, kept = feed_forward(
        normed.astype(jnp.bfloat16), up_weight, up_bias, down_weight, down_bias.astype(jnp.float32)
    )
    residual = normed + branch
    result = (
        layer_norm(residual, gain_out.astype(jnp.float32), shift_out.astype(jnp.float32))
        * live_mask
    )
    return (result, (summed, residual, kept))


def layer_backward(result_cot, live_mask, params, tables, saved):
    gain_mix, shift_mix, up_weight, up_bias, down_weight, down_bias, gain_out, shift_out = params
    own_pair, pair_full, wide_table = tables
    summed, residual, kept = saved
    result_value, out_pull = jax.vjp(
        layer_norm, residual, gain_out.astype(jnp.float32), shift_out.astype(jnp.float32)
    )
    resid_grad, gainout_grad, shiftout_grad = out_pull(result_cot * live_mask)
    branch_cot = resid_grad.astype(jnp.bfloat16)
    downbias_grad = jnp.sum(branch_cot, axis=(0, 1), dtype=jnp.float32)
    normed_grad, large_grads = feed_backward(branch_cot, kept)
    normed_grad = normed_grad + resid_grad
    normed_value, mix_pull = jax.vjp(
        layer_norm, summed, gain_mix.astype(jnp.float32), shift_mix.astype(jnp.float32)
    )
    summed_grad, gainmix_grad, shiftmix_grad = mix_pull(normed_grad)
    spectra_grad = spectra_backward(summed_grad.astype(jnp.bfloat16), own_pair)
    flat_grad = spectra_grad.reshape(
        spectra_grad.shape[0], spectra_grad.shape[1], 2 * spectra_grad.shape[3]
    )
    masked_grad = summed_grad + jnp.einsum(
        "rtk,dk->rtd", flat_grad, wide_table, preferred_element_type=jnp.float32
    )
    small_grads = (gainmix_grad, shiftmix_grad, downbias_grad, gainout_grad, shiftout_grad)
    return (masked_grad * live_mask, large_grads, small_grads)


def total_grads(large_grads, small_grads):
    up_grad, upbias_grad, down_grad = large_grads
    gainmix_grad, shiftmix_grad, downbias_grad, gainout_grad, shiftout_grad = small_grads
    large_total = (
        lax.psum(up_grad.astype(jnp.bfloat16), "dp").astype(jnp.float32),
        lax.psum(upbias_grad.astype(jnp.bfloat16), "dp").astype(jnp.float32),
        lax.psum(down_grad.astype(jnp.bfloat16), "dp").astype(jnp.float32),
    )
    small_total = lax.psum(
        (gainmix_grad, shiftmix_grad, downbias_grad, gainout_grad, shiftout_grad), ("dp", "mp")
    )
    return (large_total, small_total)


def on_device(
    inputs,
    pad_counts,
    gainmix_one,
    shiftmix_one,
    upweight_one,
    upbias_one,
    downweight_one,
    downbias_one,
    gainout_one,
    shiftout_one,
    gainmix_two,
    shiftmix_two,
    upweight_two,
    upbias_two,
    downweight_two,
    downbias_two,
    gainout_two,
    shiftout_two,
    cotangent,
):
    shard_size = inputs.shape[1]
    feature_width = inputs.shape[2]
    row_length = shard_size * lax.axis_size("mp")
    offset = lax.axis_index("mp") * shard_size
    cos_seq, sin_seq = fourier_table(row_length)
    pair_full = jnp.stack([cos_seq, -sin_seq], axis=1).astype(jnp.bfloat16)
    own_pair = lax.dynamic_slice_in_dim(pair_full, offset, shard_size, 0)
    cos_wid, sin_wid = fourier_table(feature_width)
    wide_table = jnp.concatenate([cos_wid, sin_wid], axis=1).astype(jnp.bfloat16)
    tables = (own_pair, pair_full, wide_table)
    position = offset + jnp.arange(shard_size, dtype=jnp.int32)
    live_mask = (position[None, :] < row_length - pad_counts[:, None]).astype(jnp.float32)[
        :, :, None
    ]
    first_params = (
        gainmix_one,
        shiftmix_one,
        upweight_one,
        upbias_one,
        downweight_one,
        downbias_one,
        gainout_one,
        shiftout_one,
    )
    second_params = (
        gainmix_two,
        shiftmix_two,
        upweight_two,
        upbias_two,
        downweight_two,
        downbias_two,
        gainout_two,
        shiftout_two,
    )
    first_out, first_saved = layer_forward(
        inputs.astype(jnp.float32), live_mask, first_params, tables
    )
    second_out, second_saved = layer_forward(first_out, live_mask, second_params, tables)
    middle_grad, second_large, second_small = layer_backward(
        cotangent.astype(jnp.float32), live_mask, second_params, tables, second_saved
    )
    input_grad, first_large, first_small = layer_backward(
        middle_grad, live_mask, first_params, tables, first_saved
    )
    both_large, both_small = total_grads(
        tuple((jnp.stack(pair_grads) for pair_grads in zip(first_large, second_large))),
        tuple((jnp.stack(pair_grads) for pair_grads in zip(first_small, second_small))),
    )
    first_large = tuple((member[0] for member in both_large))
    second_large = tuple((member[1] for member in both_large))
    first_small = tuple((member[0] for member in both_small))
    second_small = tuple((member[1] for member in both_small))
    final_out = second_out.astype(jnp.bfloat16)
    return (
        final_out,
        input_grad,
        first_small[0],
        first_small[1],
        first_large[0],
        first_large[1],
        first_large[2],
        first_small[2],
        first_small[3],
        first_small[4],
        second_small[0],
        second_small[1],
        second_large[0],
        second_large[1],
        second_large[2],
        second_small[2],
        second_small[3],
        second_small[4],
    )


def solution(mesh):
    placed = (
        P("dp", "mp", None),
        P("dp"),
        P(),
        P(),
        P(None, "mp"),
        P("mp"),
        P("mp", None),
        P(),
        P(),
        P(),
        P(),
        P(),
        P(None, "mp"),
        P("mp"),
        P("mp", None),
        P(),
        P(),
        P(),
        P("dp", "mp", None),
    )
    return jax.shard_map(
        on_device,
        mesh=mesh,
        in_specs=placed,
        out_specs=(
            P("dp", "mp", None),
            P("dp", "mp", None),
            P(),
            P(),
            P(None, "mp"),
            P("mp"),
            P("mp", None),
            P(),
            P(),
            P(),
            P(),
            P(),
            P(None, "mp"),
            P("mp"),
            P("mp", None),
            P(),
            P(),
            P(),
        ),
        check_vma=False,
    )
```

profile of v0, /device:TPU:0, one launch (start us, length us, event | category | flops | bytes accessed | tf_op | source)
XLA Modules:
  0.0 706.4 jit_solution(14929183615843400449)
XLA Ops:
  7.3 10.7 %multiply_convert_fusion.2 = (bf16[768,768]{1,0:T(8,128)(2,1)S(1)}, bf16[768,768]{1,0:T(8,128)(2,1)}) fusion(), kind=kLoop, calls=%fused_computation.58 | loop fusion | flops 7667712 | bytes 2359296 | tf_op jit(solution)/shard_map/convert.15
  34.0 41.2 %all-gather.9.cloned.1.call-done = bf16[2,512,2,768]{1,3,2,0:T(8,128)(2,1)} async-done(((bf16[2,256,2,768]{1,3,2,0:T(8,128)(2,1)}), bf16[2,512,2,768]{1,3,2,0:T(8,128)(2,1)}) %all-gather.9.cloned.1.call-update) | async-done | bytes 3145744 | tf_op jit(solution)/shard_map/all_gather | solution.py:41
  82.2 26.0 %all-gather.11.cloned.1.call-done = bf16[2,512,768]{1,2,0:T(8,128)(2,1)} async-done(((bf16[2,256,768]{1,2,0:T(8,128)(2,1)}), bf16[2,512,768]{1,2,0:T(8,128)(2,1)}) %all-gather.11.cloned.1.call-update) | async-done | bytes 1572880 | tf_op jit(solution)/shard_map/all_gather | solution.py:58
  108.2 4.9 fusion.32
  124.2 22.4 %reduce-scatter.5.cloned.1.call-done = bf16[2,256,768]{1,2,0:T(8,128)(2,1)} async-done(((bf16[2,512,768]{1,2,0:T(8,128)(2,1)}), bf16[2,256,768]{1,2,0:T(8,128)(2,1)}) %reduce-scatter.5.cloned.1.call-update) | async-done | bytes 786448 | tf_op jit(solution)/shard_map/reduce_scatter | solution.py:65
  156.6 44.4 %all-gather.13.cloned.1.call-done = bf16[2,512,2,768]{1,3,2,0:T(8,128)(2,1)} async-done(((bf16[2,256,2,768]{1,3,2,0:T(8,128)(2,1)}), bf16[2,512,2,768]{1,3,2,0:T(8,128)(2,1)}) %all-gather.13.cloned.1.call-update) | async-done | bytes 3145744 | tf_op jit(solution)/shard_map/all_gather | solution.py:41
  206.9 27.2 %all-gather.15.cloned.1.call-done = bf16[2,512,768]{1,2,0:T(8,128)(2,1)} async-done(((bf16[2,256,768]{1,2,0:T(8,128)(2,1)}), bf16[2,512,768]{1,2,0:T(8,128)(2,1)}) %all-gather.15.cloned.1.call-update) | async-done | bytes 1572880 | tf_op jit(solution)/shard_map/all_gather | solution.py:58
  234.2 4.8 fusion.25
  241.6 4.5 fusion.46
  248.3 24.1 %reduce-scatter.7.cloned.1.call-done = bf16[2,256,768]{1,2,0:T(8,128)(2,1)} async-done(((bf16[2,512,768]{1,2,0:T(8,128)(2,1)}), bf16[2,256,768]{1,2,0:T(8,128)(2,1)}) %reduce-scatter.7.cloned.1.call-update) | async-done | bytes 786448 | tf_op jit(solution)/shard_map/reduce_scatter | solution.py:65
  281.2 26.8 %all-gather.17.cloned.1.call-done = bf16[2,512,768]{1,2,0:T(8,128)(2,1)} async-done(((bf16[2,256,768]{1,2,0:T(8,128)(2,1)}), bf16[2,512,768]{1,2,0:T(8,128)(2,1)}) %all-gather.17.cloned.1.call-update) | async-done | bytes 1572880 | tf_op jit(solution)/shard_map/all_gather | solution.py:75
  308.0 9.3 %fusion.87 = (bf16[1536]{0:T(1024)(128)(2,1)}, bf16[2,512,1536]{2,1,0:T(8,128)(2,1)S(1)}) fusion(f32[2,512,1536]{2,1,0:T(8,128)} %copy-done.78, f32[1536]{0:T(1024)S(1)} %convert_element_type.202, bf16[2,512,768]{1,2,0:T(8,128)(2,1)} %all-gather.17.cloned.1.call-done, bf16[1536,768]{1,0:T(8,128)(2,1)S(1)} %copy-done), kind=kOutput, calls=%fused_computation.182 | convolution fusion | flops 2450520576 | bytes 13378560 | tf_op jit(solution)/shard_map/rtd,fd->rtf/dot_general | solution.py:77
  322.8 26.2 %reduce-scatter.9.cloned.1.call-done = bf16[2,256,768]{1,2,0:T(8,128)(2,1)} async-done(((bf16[2,512,768]{1,2,0:T(8,128)(2,1)}), bf16[2,256,768]{1,2,0:T(8,128)(2,1)}) %reduce-scatter.9.cloned.1.call-update) | async-done | bytes 786448 | tf_op jit(solution)/shard_map/reduce_scatter | solution.py:86
  356.3 27.2 %all-gather.19.cloned.1.call-done = bf16[2,512,768]{1,2,0:T(8,128)(2,1)} async-done(((bf16[2,256,768]{1,2,0:T(8,128)(2,1)}), bf16[2,512,768]{1,2,0:T(8,128)(2,1)}) %all-gather.19.cloned.1.call-update) | async-done | bytes 1572880 | tf_op jit(solution)/shard_map/all_gather | solution.py:53
  392.8 27.1 %all-gather.21.cloned.1.call-done = bf16[2,512,768]{1,2,0:T(8,128)(2,1)} async-done(((bf16[2,256,768]{1,2,0:T(8,128)(2,1)}), bf16[2,512,768]{1,2,0:T(8,128)(2,1)}) %all-gather.21.cloned.1.call-update) | async-done | bytes 1572880 | tf_op jit(solution)/shard_map/all_gather | solution.py:75
  419.9 9.8 %fusion.88 = (bf16[1536]{0:T(1024)(128)(2,1)}, bf16[2,512,1536]{2,1,0:T(8,128)(2,1)S(1)}) fusion(f32[2,512,1536]{2,1,0:T(8,128)} %copy-done.77, f32[1536]{0:T(1024)S(1)} %copy-done.53, bf16[2,512,768]{1,2,0:T(8,128)(2,1)} %all-gather.21.cloned.1.call-done, bf16[1536,768]{1,0:T(8,128)(2,1)} %param.25), kind=kOutput, calls=%fused_computation.183 | convolution fusion | flops 2450520576 | bytes 13378560 | tf_op jit(solution)/shard_map/rtd,fd->rtf/dot_general | solution.py:77
  436.5 5.8 fusion.15
  442.3 8.7 %fusion.17 = bf16[1,1536,768]{2,1,0:T(8,128)(2,1)} fusion(bf16[2,512,768]{1,2,0:T(8,128)(2,1)S(1)} %copy-done.75, f32[2,512,1536]{2,1,0:T(8,128)} %copy-done.78, f32[1536]{0:T(1024)S(1)} %copy-done.56), kind=kOutput, calls=%fused_computation.34 | convolution fusion | flops 2432827392 | bytes 10229760 | tf_op jit(solution)/shard_map/rtf,rtd->fd/dot_general | solution.py:76
  451.0 10.3 %reduce-scatter.11.cloned.1.call-done = bf16[2,256,768]{1,2,0:T(8,128)(2,1)} async-done(((bf16[2,512,768]{1,2,0:T(8,128)(2,1)}), bf16[2,256,768]{1,2,0:T(8,128)(2,1)}) %reduce-scatter.11.cloned.1.call-update) | async-done | bytes 786448 | tf_op jit(solution)/shard_map/reduce_scatter | solution.py:86
  467.6 7.8 %fusion.16 = bf16[1,1536,768]{2,1,0:T(8,128)(2,1)S(1)} fusion(bf16[2,512,768]{1,2,0:T(8,128)(2,1)} %all-gather.21.cloned.1.call-done, f32[2,512,1536]{2,1,0:T(8,128)} %copy-done.77, f32[1536]{0:T(1024)S(1)} %copy-done.54), kind=kOutput, calls=%fused_computation.33 | convolution fusion | flops 2432827392 | bytes 10229760 | tf_op jit(solution)/shard_map/rtf,rtd->fd/dot_general | solution.py:76
  487.5 34.7 %psum.59 = bf16[2,1536]{1,0:T(2,128)(2,1)S(1)} all-reduce(bf16[2,1536]{1,0:T(2,128)(2,1)S(1)} %pad_maximum_fusion.4), channel_id=1, replica_groups=mesh['dp'=16,'mp'=2] {'dp'}, use_global_device_ids=true, to_apply=%region_29.30 | all-reduce | flops 3072 | bytes 12288 | tf_op jit(solution)/shard_map/psum | solution.py:146
  522.9 39.3 %all-reduce = (f32[2,768]{1,0:T(2,128)S(1)}, f32[2,768]{1,0:T(2,128)S(1)}, f32[2,768]{1,0:T(2,128)S(1)}, f32[2,768]{1,0:T(2,128)S(1)}, f32[2,768]{1,0:T(2,128)S(1)}) all-reduce(f32[2,768]{1,0:T(2,128)S(1)} %pad_maximum_fusion.2, f32[2,768]{1,0:T(2,128)S(1)} %pad_maximum_fusion.3, ...), channel_id=1, replica_groups=mesh['dp'=16,'mp'=2] {'dp','mp'}, use_global_device_ids=true, to_apply=%region_22.23 | all-reduce | flops 7680 | bytes 61440 | tf_op jit(solution)/shard_map/psum | solution.py:149
  573.5 112.5 %all-reduce.4.cloned.1.call-done = (bf16[2,768,1536]{2,1,0:T(8,128)(2,1)}, bf16[2,1536,768]{2,1,0:T(8,128)(2,1)}) async-done(((bf16[2,768,1536]{2,1,0:T(8,128)(2,1)}, bf16[2,1536,768]{2,1,0:T(8,128)(2,1)}), (bf16[2,768,1536]{2,1,0:T(8,128)(2,1)}, bf16[2,1536,768]{2,1,0:T(8,128)(2,1)})) %all-reduce.4.cloned.1.call-update) | async-done | bytes 9437200 | tf_op jit(solution)/shard_map/psum | solution.py:145
  689.8 4.6 slice_bitcast_fusion.1
  (296 shorter events, 130.8 us)
Async XLA Ops:
  7.2 234.4 %copy-start = (bf16[1536,768]{1,0:T(8,128)(2,1)S(1)}, bf16[1536,768]{1,0:T(8,128)(2,1)}, u32[]{:S(2)}) copy-start(bf16[1536,768]{1,0:T(8,128)(2,1)} %param.33) | copy-start | bytes 7077892
  7.2 68.0 %all-gather.9.cloned.1.call-start = ((), (), s32[]{:S(2)}) async-start(), calls=%async_computation.4 | async-start | bytes 4718592 | tf_op jit(solution)/shard_map/all_gather | solution.py:41
  18.0 131.6 %copy-start.20 = (bf16[768,768]{1,0:T(8,128)(2,1)}, bf16[768,768]{1,0:T(8,128)(2,1)S(1)}, u32[]{:S(2)}) copy-start(bf16[768,768]{1,0:T(8,128)(2,1)S(1)} %get-tuple-element.97) | copy-start | bytes 3538948
  20.8 54.4 %copy-start.28 = (f32[2,256]{1,0:T(2,128)}, f32[2,256]{1,0:T(2,128)S(1)}, u32[]{:S(2)}) copy-start(f32[2,256]{1,0:T(2,128)S(1)} %compare_convert_fusion) | copy-start | bytes 6148
  27.4 80.7 %all-gather.11.cloned.1.call-start = ((), (), s32[]{:S(2)}) async-start(), calls=%async_computation.5 | async-start | bytes 2359296 | tf_op jit(solution)/shard_map/all_gather | solution.py:58
  80.8 65.7 %reduce-scatter.5.cloned.1.call-start = ((), (), s32[]{:S(2)}) async-start(), calls=%async_computation.6 | async-start | bytes 2359296 | tf_op jit(solution)/shard_map/reduce_scatter | solution.py:65
  120.3 80.7 %all-gather.13.cloned.1.call-start = ((), (), s32[]{:S(2)}) async-start(), calls=%async_computation.7 | async-start | bytes 4718592 | tf_op jit(solution)/shard_map/all_gather | solution.py:41
  155.9 45.1 %copy-start.25 = (bf16[256,2,512,1]{2,0,1,3:T(8,128)(2,1)S(1)}, bf16[256,2,512,1]{2,0,1,3:T(8,128)(2,1)}, u32[]{:S(2)}) copy-start(bf16[256,2,512,1]{2,0,1,3:T(8,128)(2,1)} %fusion.72) | copy-start | bytes 1572868
  155.9 45.1 %copy-start.32 = (f32[2,256]{1,0:T(2,128)S(1)}, f32[2,256]{1,0:T(2,128)}, u32[]{:S(2)}) copy-start(f32[2,256]{1,0:T(2,128)} %copy-done.31) | copy-start | bytes 6148
  155.9 45.1 %copy-start.47 = (f32[768]{0:T(1024)S(1)}, f32[768]{0:T(1024)}, u32[]{:S(2)}) copy-start(f32[768]{0:T(1024)} %convert_element_type.195) | copy-start | bytes 9220
  155.9 45.1 %copy-start.50 = (f32[2,256]{1,0:T(2,128)S(1)}, f32[2,256]{1,0:T(2,128)}, u32[]{:S(2)}) copy-start(f32[2,256]{1,0:T(2,128)} %copy-done.49) | copy-start | bytes 6148
  155.9 45.1 %copy-start.61 = (f32[768]{0:T(1024)S(1)}, f32[768]{0:T(1024)}, u32[]{:S(2)}) copy-start(f32[768]{0:T(1024)} %convert_element_type.196) | copy-start | bytes 9220
  155.9 78.2 %all-gather.15.cloned.1.call-start = ((), (), s32[]{:S(2)}) async-start(), calls=%async_computation.8 | async-start | bytes 2359296 | tf_op jit(solution)/shard_map/all_gather | solution.py:58
  206.9 65.6 %reduce-scatter.7.cloned.1.call-start = ((), (), s32[]{:S(2)}) async-start(), calls=%async_computation.9 | async-start | bytes 2359296 | tf_op jit(solution)/shard_map/reduce_scatter | solution.py:65
  206.9 101.0 %copy-start.55 = (f32[1536]{0:T(1024)}, f32[1536]{0:T(1024)S(1)}, u32[]{:S(2)}) copy-start(f32[1536]{0:T(1024)S(1)} %convert_element_type.202) | copy-start | bytes 18436
  246.2 61.8 %all-gather.17.cloned.1.call-start = ((), (), s32[]{:S(2)}) async-start(), calls=%async_computation.10 | async-start | bytes 2359296 | tf_op jit(solution)/shard_map/all_gather | solution.py:75
  280.6 68.4 %reduce-scatter.9.cloned.1.call-start = ((), (), s32[]{:S(2)}) async-start(), calls=%async_computation.11 | async-start | bytes 2359296 | tf_op jit(solution)/shard_map/reduce_scatter | solution.py:86
  322.7 60.8 %all-gather.19.cloned.1.call-start = ((), (), s32[]{:S(2)}) async-start(), calls=%async_computation.12 | async-start | bytes 2359296 | tf_op jit(solution)/shard_map/all_gather | solution.py:53
  356.3 63.6 %all-gather.21.cloned.1.call-start = ((), (), s32[]{:S(2)}) async-start(), calls=%async_computation.13 | async-start | bytes 2359296 | tf_op jit(solution)/shard_map/all_gather | solution.py:75
  392.6 68.8 %reduce-scatter.11.cloned.1.call-start = ((), (), s32[]{:S(2)}) async-start(), calls=%async_computation.14 | async-start | bytes 2359296 | tf_op jit(solution)/shard_map/reduce_scatter | solution.py:86
  435.1 130.2 %all-gather.23.cloned.1.call-start = ((), (), s32[]{:S(2)}) async-start(), calls=%async_computation.15 | async-start | bytes 2359296 | tf_op jit(solution)/shard_map/all_gather | solution.py:53
  467.3 218.7 %all-reduce.4.cloned.1.call-start = ((), (), s32[]{:S(2)}) async-start(), calls=%async_computation.16 | async-start | bytes 18874368 | tf_op jit(solution)/shard_map/psum | solution.py:145
  485.1 37.8 %copy-start.45 = (f32[768]{0:T(1024)S(1)}, f32[768]{0:T(1024)}, u32[]{:S(2)}) copy-start(f32[768]{0:T(1024)} %get-tuple-element.36) | copy-start | bytes 9220
  485.1 80.2 %copy-start.27 = (bf16[256,2,512,1]{2,0,1,3:T(8,128)(2,1)S(1)}, bf16[256,2,512,1]{2,0,1,3:T(8,128)(2,1)}, u32[]{:S(2)}) copy-start(bf16[256,2,512,1]{2,0,1,3:T(8,128)(2,1)} %fusion.72) | copy-start | bytes 1572868
  (73 other events, 474.4 us)
Sparse Core Ops, SparseCore 0:
  27.6 47.5 all-gather.8
  81.0 27.1 all-gather.10
  120.4 26.0 reduce-scatter.4
  156.1 44.8 all-gather.12
  207.0 27.1 all-gather.14
  246.3 26.0 reduce-scatter.6
  280.7 27.1 all-gather.16
  322.9 26.0 reduce-scatter.8
  356.3 27.1 all-gather.18
  392.7 27.1 all-gather.20
  435.3 26.0 reduce-scatter.10
  467.5 27.1 all-gather.22
  499.5 186.4 all-reduce.3
where the time goes:
time: 715 us; the launch traced here: 706 us
  waiting for transfers between devices  416 us (58%)
  matrix products  95.8 us (13%)
  blocking collectives  74 us (10%)
  other arithmetic  57 us (8%)
  local copies, waits for them, and re-layouts  47 us (7%)
  between operations  15.2 us (2%)
    psum x1, waiting for transfers between devices, total_grads(): lax.psum(up_grad.astype(jnp.bfloat16), 'dp').astype(jnp.float32)  113 us
    all_gather x2, waiting for transfers between devices, spectra_forward(): lax.all_gather(spectra, 'mp', axis=1, tiled=True)  85.6 us
    all_gather x2, waiting for transfers between devices, feed_backward(): cot_rows = lax.all_gather(branch_cot, 'mp', axis=1, tiled=True)  53.9 us
    all_gather x2, waiting for transfers between devices, feed_forward(): gathered = lax.all_gather(normed_low, 'mp', axis=1, tiled=True)  53.2 us
    reduce_scatter x2, waiting for transfers between devices, feed_forward(): lax.psum_scatter(partial_sum.astype(jnp.bfloat16), 'mp', scatter_dimensio...  46.5 us
    psum x1, blocking collectives, total_grads(): lax.psum((gainmix_grad, shiftmix_grad, downbias_grad, gainout_grad, shift...  39.3 us
    reduce_scatter x2, waiting for transfers between devices, feed_backward(): lax.psum_scatter(partial_grad.astype(jnp.bfloat16), 'mp', scatter_dimensi...  36.5 us
    psum x1, blocking collectives, total_grads(): lax.psum(upbias_grad.astype(jnp.bfloat16), 'dp').astype(jnp.float32)  34.7 us
  transfers between devices with their start and end apart: 13, of which 12 were waited for; matrix products, arithmetic and copies ran while one was open for 8% of the time, Pallas kernels for 0%

commit v1 on v0

v1 whole, which is shorter than its diff:
```python
import math

import jax
import jax.numpy as jnp
import numpy as np
from jax import lax
from jax.sharding import PartitionSpec as P

norm_eps = 1e-05
low_type = jnp.bfloat16
wide_type = jnp.float32


def fourier_table(points):
    indices = np.arange(points, dtype=np.int64)
    phases = (indices[:, None] * indices[None, :]) % points
    angles = phases.astype(np.float32) * np.float32(2.0 * math.pi / points)
    factor = np.float32(points ** (-0.5))
    return (np.cos(angles) * factor, np.sin(angles) * factor)


def dot(left, right):
    return jnp.dot(left, right, preferred_element_type=wide_type)


def dot_tn(left, right):
    return lax.dot_general(left, right, (((0,), (0,)), ((), ())), preferred_element_type=wide_type)


def dot_nt(left, right):
    return lax.dot_general(left, right, (((1,), (1,)), ((), ())), preferred_element_type=wide_type)


def normalize(activity):
    center = jnp.mean(activity, axis=-1, keepdims=True)
    centered = activity - center
    spread = jnp.mean(centered * centered, axis=-1, keepdims=True)
    inverse = lax.rsqrt(spread + norm_eps)
    return centered * inverse, inverse


def norm_backward(grad, normal, inverse, gain):
    pulled = grad * gain
    first = jnp.mean(pulled, axis=-1, keepdims=True)
    second = jnp.mean(pulled * normal, axis=-1, keepdims=True)
    return inverse * (pulled - first - normal * second)


def gate_pair(preact):
    scale = math.sqrt(2.0 / math.pi)
    square = preact * preact
    turn = jnp.tanh(scale * (preact + 0.044715 * preact * square))
    half = 0.5 * (1.0 + turn)
    slope = half + (0.5 * scale) * preact * (1.0 - turn * turn) * (1.0 + 3 * 0.044715 * square)
    return (preact * half).astype(low_type), slope.astype(low_type)


def flip_pairs(size, bit):
    return [(index, index ^ bit) for index in range(size)]


def order_halves(bit_value, mine, theirs):
    return jnp.where(
        bit_value == 0,
        jnp.concatenate([mine, theirs], axis=0),
        jnp.concatenate([theirs, mine], axis=0),
    )


def take_half(array, which):
    half = array.shape[0] // 2
    return lax.dynamic_slice_in_dim(array, which * half, half, 0)


def dp_bits():
    return [1 << level for level in range(lax.axis_size("dp").bit_length() - 1)]


def bit_of(bit):
    return (lax.axis_index("dp") // bit) % 2


def dp_swap(array, bit):
    return lax.ppermute(array, "dp", flip_pairs(lax.axis_size("dp"), bit))


def mp_swap(array):
    return lax.ppermute(array, "mp", [(0, 1), (1, 0)])


def add_low(left, right):
    return (left.astype(wide_type) + right.astype(wide_type)).astype(low_type)


def halve_over(array, bit):
    own_bit = bit_of(bit)
    received = dp_swap(take_half(array, 1 - own_bit), bit)
    return add_low(take_half(array, own_bit), received)


def gather_over(array, bit):
    return order_halves(bit_of(bit), array, dp_swap(array, bit))


def fetch_other(weight):
    bits = dp_bits()[:2]
    piece = weight
    for bit in bits:
        piece = take_half(piece, bit_of(bit))
    piece = mp_swap(piece)
    for bit in bits[::-1]:
        piece = gather_over(piece, bit)
    return piece


def gathered_weights(up_weight, up_bias, down_weight):
    if lax.axis_size("mp") == 2:
        return (
            (up_weight, up_bias, down_weight),
            (fetch_other(up_weight), mp_swap(up_bias), fetch_other(down_weight)),
        )
    return (
        (
            lax.all_gather(up_weight, "mp", axis=1, tiled=True),
            lax.all_gather(up_bias, "mp", axis=0, tiled=True),
            lax.all_gather(down_weight, "mp", axis=0, tiled=True),
        ),
    )


def total_large(parts, hidden_axis):
    bits = dp_bits()
    if len(parts) == 2:
        own, other = parts
        other = halve_over(other, bits[0])
        own = halve_over(own, bits[0])
        own = add_low(own, mp_swap(other))
    else:
        own = lax.psum_scatter(parts[0], "mp", scatter_dimension=hidden_axis, tiled=True)
        own = halve_over(own, bits[0])
    for bit in bits[1:]:
        own = halve_over(own, bit)
    for bit in bits[::-1]:
        own = gather_over(own, bit)
    return own.astype(wide_type)


def total_small(vector):
    for bit in dp_bits():
        vector = vector + dp_swap(vector, bit)
    if lax.axis_size("mp") == 2:
        return vector + mp_swap(vector)
    return lax.psum(vector, "mp")


def exchange_rows(array):
    if lax.axis_size("mp") == 2:
        mine = lax.axis_index("mp")
        own = lax.dynamic_index_in_dim(array, mine, 0, keepdims=False)
        given = lax.dynamic_index_in_dim(array, 1 - mine, 0, keepdims=False)
        return jnp.concatenate([own, mp_swap(given)], axis=0)
    return lax.all_to_all(array, "mp", split_axis=0, concat_axis=1, tiled=True)[0]


def return_rows(array):
    if lax.axis_size("mp") == 2:
        mine = lax.axis_index("mp")
        half = array.shape[0] // 2
        own, received = array[:half], mp_swap(array[half:])
        return jnp.where(mine == 0, jnp.stack([own, received]), jnp.stack([received, own]))
    return lax.all_to_all(array[None], "mp", split_axis=1, concat_axis=0, tiled=True)


def layer_forward(layer_in, live_mask, params, weights, tables):
    gain_mix, shift_mix, down_bias, gain_out, shift_out = params
    pair_table, wide_table = tables
    width = layer_in.shape[1]
    masked = layer_in * live_mask
    spectra = dot(masked.astype(low_type), wide_table).astype(low_type)
    stacked = jnp.concatenate([spectra[:, :width], spectra[:, width:]], axis=0)
    summed = masked + dot(pair_table, stacked)
    normal, inverse = normalize(summed)
    normed = normal * gain_mix + shift_mix
    normed_low = normed.astype(low_type)
    branch = down_bias
    kept = []
    for up_weight, up_bias, down_weight in weights:
        hidden, slope = gate_pair(dot(normed_low, up_weight) + up_bias.astype(wide_type))
        branch = branch + dot(hidden, down_weight)
        kept.append((hidden, slope))
    residual = normed + branch
    out_normal, out_inverse = normalize(residual)
    result = (out_normal * gain_out + shift_out) * live_mask
    return result, (summed, normed_low, residual, kept)


def layer_backward(result_cot, live_mask, params, weights, tables, saved):
    gain_mix, shift_mix, down_bias, gain_out, shift_out = params
    pair_table, wide_table = tables
    summed, normed_low, residual, kept = saved
    length = summed.shape[0]
    out_grad = result_cot * live_mask
    out_normal, out_inverse = normalize(residual)
    resid_grad = norm_backward(out_grad, out_normal, out_inverse, gain_out)
    gainout_grad = jnp.sum(out_grad * out_normal, axis=0)
    shiftout_grad = jnp.sum(out_grad, axis=0)
    branch_cot = resid_grad.astype(low_type)
    downbias_grad = jnp.sum(branch_cot, axis=0, dtype=wide_type)
    normed_grad = resid_grad
    up_parts, bias_parts, down_parts = [], [], []
    for (up_weight, up_bias, down_weight), (hidden, slope) in zip(weights[::-1], kept[::-1]):
        preact_cot = (dot_nt(branch_cot, down_weight) * slope.astype(wide_type)).astype(low_type)
        down_parts.append(dot_tn(hidden, branch_cot).astype(low_type))
        up_parts.append(dot_tn(normed_low, preact_cot).astype(low_type))
        bias_parts.append(jnp.sum(preact_cot, axis=0, dtype=wide_type))
        normed_grad = normed_grad + dot_nt(preact_cot, up_weight)
    normal, inverse = normalize(summed)
    summed_grad = norm_backward(normed_grad, normal, inverse, gain_mix)
    gainmix_grad = jnp.sum(normed_grad * normal, axis=0)
    shiftmix_grad = jnp.sum(normed_grad, axis=0)
    summed_low = summed_grad.astype(low_type)
    flat_grad = jnp.concatenate(
        [
            dot_tn(pair_table[:, :length], summed_low).astype(low_type),
            dot_tn(pair_table[:, length:], summed_low).astype(low_type),
        ],
        axis=1,
    )
    masked_grad = (summed_grad + dot_nt(flat_grad, wide_table)) * live_mask
    small = [gainmix_grad, shiftmix_grad, downbias_grad, gainout_grad, shiftout_grad]
    return masked_grad, (up_parts[::-1], down_parts[::-1]), small, bias_parts[::-1]


def on_device(*arguments):
    inputs, pad_counts = arguments[:2]
    layer_args = (arguments[2:10], arguments[10:18])
    cotangent = arguments[18]
    mp_count = lax.axis_size("mp")
    mine = lax.axis_index("mp")
    feature_width = inputs.shape[2]
    row_length = inputs.shape[1] * mp_count
    cos_seq, sin_seq = fourier_table(row_length)
    pair_full = np.concatenate([cos_seq, -sin_seq], axis=1)
    turned = 1 - 2 * ((np.arange(row_length)[:, None] + np.arange(2 * row_length)[None, :]) % 2)
    position = jnp.arange(row_length, dtype=jnp.int32)
    if mp_count == 2:
        pair_table = lax.dynamic_index_in_dim(
            jnp.asarray(np.stack([pair_full, pair_full * turned]), low_type), mine, 0, False
        )
        position = (position + mine * inputs.shape[1]) % row_length
    else:
        pair_table = jnp.asarray(pair_full, low_type)
    wide_table = jnp.asarray(np.concatenate(fourier_table(feature_width), axis=1), low_type)
    tables = (pair_table, wide_table)
    pads = lax.dynamic_index_in_dim(pad_counts, mine, 0, False)
    live_mask = (position < row_length - pads).astype(wide_type)[:, None]
    row_in = exchange_rows(inputs)
    row_cot = exchange_rows(cotangent)
    weights, params = [], []
    for gain_mix, shift_mix, up_weight, up_bias, down_weight, down_bias, gain_out, shift_out in (
        layer_args
    ):
        weights.append(gathered_weights(up_weight, up_bias, down_weight))
        params.append(
            tuple(
                member.astype(wide_type)
                for member in (gain_mix, shift_mix, down_bias, gain_out, shift_out)
            )
        )
    current = row_in.astype(wide_type)
    saved = []
    for level in range(2):
        current, kept = layer_forward(current, live_mask, params[level], weights[level], tables)
        saved.append(kept)
    final_out = return_rows(current.astype(low_type))
    grad = row_cot.astype(wide_type)
    large, small, bias = [None] * 2, [None] * 2, [None] * 2
    for level in (1, 0):
        grad, parts, small[level], bias[level] = layer_backward(
            grad, live_mask, params[level], weights[level], tables, saved[level]
        )
        large[level] = (total_large(parts[0], 1), total_large(parts[1], 0))
    input_grad = return_rows(grad.astype(low_type)).astype(wide_type)
    hidden_own = layer_args[0][3].shape[0]
    pieces = []
    for level in range(2):
        pieces.extend(small[level])
        absolute = (
            bias[level][0]
            if mp_count != 2
            else order_halves(mine, bias[level][0], bias[level][1])
        )
        pieces.append(absolute)
    vector = total_small(jnp.concatenate(pieces))
    results = [final_out, input_grad]
    offset = 0
    for level in range(2):
        vectors = []
        for _ in range(5):
            vectors.append(vector[offset : offset + feature_width])
            offset += feature_width
        bias_total = lax.dynamic_slice_in_dim(
            vector, offset + mine * hidden_own, hidden_own, 0
        )
        offset += hidden_own * mp_count
        gainmix, shiftmix, downbias, gainout, shiftout = vectors
        up_total, down_total = large[level]
        results += [gainmix, shiftmix, up_total, bias_total, down_total, downbias, gainout, shiftout]
    return tuple(results)


def solution(mesh):
    layer_specs = (P(), P(), P(None, "mp"), P("mp"), P("mp", None), P(), P(), P())
    rows = P("dp", "mp", None)
    return jax.shard_map(
        on_device,
        mesh=mesh,
        in_specs=(rows, P("dp"), *layer_specs, *layer_specs, rows),
        out_specs=(rows, rows, *layer_specs, *layer_specs),
        check_vma=False,
    )
```

time: 715 us -> 511 us (0.71)
  waiting for transfers between devices: 416 us -> 275 us
  blocking collectives: 74 us -> 0 us
  starting transfers between devices: 1.74 us -> 66.7 us
  local copies, waits for them, and re-layouts: 47 us -> 26.7 us
  other arithmetic: 57 us -> 40.3 us
  between operations: 15.2 us -> 3.53 us
    ppermute x0 -> x63, waiting for transfers between devices: none -> 275 us  [the longest x48 139 us: dp_swap(): return lax.ppermute(array, 'dp', flip_pairs(lax.axis_size('dp'), bit))]
    all_gather x8 -> x0, waiting for transfers between devices: 220 us -> none  [the longest x2 85.6 us: spectra_forward(): lax.all_gather(spectra, 'mp', axis=1, tiled=True)]
    psum x1 -> x0, waiting for transfers between devices: 113 us -> none  [total_grads(): lax.psum(up_grad.astype(jnp.bfloat16), 'dp').astype(jnp.float32)]
    reduce_scatter x4 -> x0, waiting for transfers between devices: 83 us -> none  [the longest x2 46.5 us: feed_forward(): lax.psum_scatter(partial_sum.astype(jnp.bfloat16), 'mp', scatter_dimensio...]
    psum x2 -> x0, blocking collectives: 74 us -> none  [the longest x1 39.3 us: total_grads(): lax.psum((gainmix_grad, shiftmix_grad, downbias_grad, gainout_grad, shift...]
    ppermute x0 -> x63, starting transfers between devices: none -> 66.7 us  [the longest x48 47 us: dp_swap(): return lax.ppermute(array, 'dp', flip_pairs(lax.axis_size('dp'), bit))]
    unnamed x172 -> x160, local copies, waits for them, and re-layouts: 29.1 us -> 6.54 us
    another operation x10 -> x0, other arithmetic: 20.6 us -> none
  transfers between devices with their start and end apart: 13 -> 63, of which waited for: 12 -> 26; matrix products, arithmetic and copies ran while one was open for 8% -> 18% of each run, Pallas kernels for 0% -> 0%
where the time goes in v1:
time: 511 us; the launch traced here: 503 us
  waiting for transfers between devices  275 us (54%)
  matrix products  91.1 us (18%)
  starting transfers between devices  66.7 us (13%)
  other arithmetic  40.3 us (8%)
  local copies, waits for them, and re-layouts  26.7 us (5%)
    ppermute x48, waiting for transfers between devices, dp_swap(): return lax.ppermute(array, 'dp', flip_pairs(lax.axis_size('dp'), bit))  139 us
    ppermute x15, waiting for transfers between devices, mp_swap(): return lax.ppermute(array, 'mp', [(0, 1), (1, 0)])  136 us
    ppermute x48, starting transfers between devices, dp_swap(): return lax.ppermute(array, 'dp', flip_pairs(lax.axis_size('dp'), bit))  47 us
    dot_general x12, matrix products, dot_nt(): lax.dot_general(left, right, (((1,), (1,)), ((), ())), preferred_element_...  44.7 us
    dot_general x12, matrix products, dot(): return jnp.dot(left, right, preferred_element_type=wide_type)  23.8 us
    dot_general x8, matrix products, dot_tn(): lax.dot_general(left, right, (((0,), (0,)), ((), ())), preferred_element_...  22.5 us
    ppermute x15, starting transfers between devices, mp_swap(): return lax.ppermute(array, 'mp', [(0, 1), (1, 0)])  19.7 us
    dynamic_slice x24, local copies, waits for them, and re-layouts, take_half(): return lax.dynamic_slice_in_dim(array, which * half, half, 0)  12.8 us
  transfers between devices with their start and end apart: 63, of which 26 were waited for; matrix products, arithmetic and copies ran while one was open for 18% of the time, Pallas kernels for 0%

profile of v1, /device:TPU:0, one launch (start us, length us, event | category | flops | bytes accessed | tf_op | source)
XLA Modules:
  0.0 503.4 jit_solution(7187369261930950841)
XLA Ops:
  23.6 18.8 %collective-permute-done = bf16[256,768]{1,0:T(8,128)(2,1)} collective-permute-done((bf16[256,768]{1,0:T(8,128)(2,1)}, bf16[256,768]{1,0:T(8,128)(2,1)}, u32[]{:S(2)}, u32[]{:S(2)}) %collective-permute-start) | collective-permute-done | bytes 393248 | tf_op jit(solution)/shard_map/ppermute | solution.py:88
  51.4 16.1 %collective-permute-done.1 = bf16[192,1536]{1,0:T(8,128)(2,1)S(1)} collective-permute-done((bf16[192,1536]{1,0:T(8,128)(2,1)S(1)}, bf16[192,1536]{1,0:T(8,128)(2,1)S(1)}, u32[]{:S(2)}, u32[]{:S(2)}) %collective-permute-start.1) | collective-permute-done | bytes 589856 | tf_op jit(solution)/shard_map/ppermute | solution.py:88
  70.3 13.5 %collective-permute-done.2 = bf16[192,1536]{1,0:T(8,128)(2,1)S(1)} collective-permute-done((bf16[192,1536]{1,0:T(8,128)(2,1)S(1)}, bf16[192,1536]{1,0:T(8,128)(2,1)S(1)}, u32[]{:S(2)}, u32[]{:S(2)}) %collective-permute-start.2) | collective-permute-done | bytes 589856 | tf_op jit(solution)/shard_map/ppermute | solution.py:84
  87.8 8.3 %collective-permute-done.6 = bf16[384,768]{1,0:T(8,128)(2,1)S(1)} collective-permute-done((bf16[384,768]{1,0:T(8,128)(2,1)}, bf16[384,768]{1,0:T(8,128)(2,1)S(1)}, u32[]{:S(2)}, u32[]{:S(2)}) %collective-permute-start.6) | collective-permute-done | bytes 589856 | tf_op jit(solution)/shard_map/ppermute | solution.py:84
  99.8 18.2 %collective-permute-done.9 = bf16[192,1536]{1,0:T(8,128)(2,1)S(1)} collective-permute-done((bf16[192,1536]{1,0:T(8,128)(2,1)S(1)}, bf16[192,1536]{1,0:T(8,128)(2,1)S(1)}, u32[]{:S(2)}, u32[]{:S(2)}) %collective-permute-start.9) | collective-permute-done | bytes 589856 | tf_op jit(solution)/shard_map/ppermute | solution.py:84
  157.0 5.6 %convert_reduce_fusion = (f32[1536]{0:T(1024)}, bf16[512,1536]{1,0:T(8,128)(2,1)S(1)}) fusion(f32[512,1536]{1,0:T(8,128)S(1)} %convolution_add_fusion, bf16[512,768]{1,0:T(8,128)(2,1)S(1)} %get-tuple-element.35, bf16[768,768]{1,0:T(8,128)(2,1)S(1)} %collective-permute-done.14, bf16[768,768]{1,0:T(8,128)(2,1)S(1)} %maximum_select_fusion.11, pred[]{:T(512)S(6)} %eq.94), kind=kOutput, calls=%fused_computation.16 | convolution fusion | flops 1235089920 | bytes 7870465 | tf_op jit(solution)/shard_map/dot_general | solution.py:31
  169.8 4.6 fusion.32
  174.4 5.8 %multiply_reduce_fusion.2 = (f32[768]{0:T(1024)S(1)}, f32[512]{0:T(512)S(1)}, f32[512]{0:T(512)S(1)}, f32[768]{0:T(1024)S(1)}, f32[512,768]{1,0:T(8,128)}) fusion(f32[512,768]{1,0:T(8,128)S(1)} %copy-done.5, f32[512]{0:T(512)S(1)} %copy-done.48, f32[512]{0:T(512)S(1)} %copy-done.37, f32[768]{0:T(1024)S(1)} %copy-done.44, f32[512]{0:T(512)S(1)} %copy-done.39, ...), kind=kOutput, calls=%fused_computation.87 | convolution fusion | flops 1012528640 | bytes 9587712 | tf_op jit(solution)/shard_map/dot_general | solution.py:31
  201.9 5.0 convert_reduce_fusion.2
  213.9 4.5 fusion.33
  218.5 5.2 %fusion.17 = bf16[512,768]{1,0:T(8,128)(2,1)} fusion(f32[512,768]{1,0:T(8,128)} %subtract_multiply_fusion, f32[512,768]{1,0:T(8,128)} %fusion.33, bf16[768,768]{1,0:T(8,128)(2,1)} %constant.404, f32[512]{0:T(512)S(1)} %copy-done.40, bf16[512,1024]{1,0:T(8,128)(2,1)} %dynamic-slice_bitcast_fusion), kind=kOutput, calls=%fused_computation.80 | convolution fusion | flops 1008992256 | bytes 7211008 | tf_op jit(solution)/shard_map/dot_general | solution.py:31
  252.5 22.6 %collective-permute-done.55 = bf16[768,768]{1,0:T(8,128)(2,1)S(1)} collective-permute-done((bf16[768,768]{1,0:T(8,128)(2,1)S(1)}, bf16[768,768]{1,0:T(8,128)(2,1)S(1)}, u32[]{:S(2)}, u32[]{:S(2)}) %collective-permute-start.55) | collective-permute-done | bytes 1179680 | tf_op jit(solution)/shard_map/ppermute | solution.py:88
  277.7 22.6 %collective-permute-done.45 = bf16[384,1536]{1,0:T(8,128)(2,1)S(1)} collective-permute-done((bf16[384,1536]{1,0:T(8,128)(2,1)S(1)}, bf16[384,1536]{1,0:T(8,128)(2,1)S(1)}, u32[]{:S(2)}, u32[]{:S(2)}) %collective-permute-start.45) | collective-permute-done | bytes 1179680 | tf_op jit(solution)/shard_map/ppermute | solution.py:88
  303.9 21.7 %collective-permute-done.35 = bf16[768,768]{1,0:T(8,128)(2,1)S(1)} collective-permute-done((bf16[768,768]{1,0:T(8,128)(2,1)S(1)}, bf16[768,768]{1,0:T(8,128)(2,1)S(1)}, u32[]{:S(2)}, u32[]{:S(2)}) %collective-permute-start.35) | collective-permute-done | bytes 1179680 | tf_op jit(solution)/shard_map/ppermute | solution.py:88
  328.3 30.2 %collective-permute-done.25 = bf16[384,1536]{1,0:T(8,128)(2,1)S(1)} collective-permute-done((bf16[384,1536]{1,0:T(8,128)(2,1)S(1)}, bf16[384,1536]{1,0:T(8,128)(2,1)S(1)}, u32[]{:S(2)}, u32[]{:S(2)}) %collective-permute-start.25) | collective-permute-done | bytes 1179680 | tf_op jit(solution)/shard_map/ppermute | solution.py:88
  365.2 8.2 %collective-permute-done.26 = bf16[192,1536]{1,0:T(8,128)(2,1)S(1)} collective-permute-done((bf16[192,1536]{1,0:T(8,128)(2,1)S(1)}, bf16[192,1536]{1,0:T(8,128)(2,1)S(1)}, u32[]{:S(2)}, u32[]{:S(2)}) %collective-permute-start.26) | collective-permute-done | bytes 589856 | tf_op jit(solution)/shard_map/ppermute | solution.py:84
  378.8 5.5 %collective-permute-start.48 = (bf16[48,1536]{1,0:T(8,128)(2,1)S(1)}, bf16[48,1536]{1,0:T(8,128)(2,1)S(1)}, u32[]{:S(2)}, u32[]{:S(2)}) collective-permute-start(bf16[48,1536]{1,0:T(8,128)(2,1)S(1)} %constant_dynamic-slice_fusion.5), channel_id=1, source_target_pairs={{0,16},{2,18},{4,20},{6,22},{8,24},{10,26},{12,28},{14,30},{16,0},... | collective-permute-start | bytes 442376 | tf_op jit(solution)/shard_map/ppermute | solution.py:84
  384.2 7.1 %collective-permute-done.37 = bf16[192,768]{1,0:T(8,128)(2,1)S(1)} collective-permute-done((bf16[192,768]{1,0:T(8,128)(2,1)S(1)}, bf16[192,768]{1,0:T(8,128)(2,1)S(1)}, u32[]{:S(2)}, u32[]{:S(2)}) %collective-permute-start.37) | collective-permute-done | bytes 294944 | tf_op jit(solution)/shard_map/ppermute | solution.py:84
  398.8 13.3 %collective-permute-done.28 = bf16[48,1536]{1,0:T(8,128)(2,1)S(1)} collective-permute-done((bf16[48,1536]{1,0:T(8,128)(2,1)S(1)}, bf16[48,1536]{1,0:T(8,128)(2,1)S(1)}, u32[]{:S(2)}, u32[]{:S(2)}) %collective-permute-start.28) | collective-permute-done | bytes 147488 | tf_op jit(solution)/shard_map/ppermute | solution.py:84
  415.2 9.1 %collective-permute-done.29 = bf16[48,1536]{1,0:T(8,128)(2,1)S(1)} collective-permute-done((bf16[48,1536]{1,0:T(8,128)(2,1)S(1)}, bf16[48,1536]{1,0:T(8,128)(2,1)S(1)}, u32[]{:S(2)}, u32[]{:S(2)}) %collective-permute-start.29) | collective-permute-done | bytes 147488 | tf_op jit(solution)/shard_map/ppermute | solution.py:84
  428.0 8.3 %collective-permute-done.30 = bf16[96,1536]{1,0:T(8,128)(2,1)S(1)} collective-permute-done((bf16[96,1536]{1,0:T(8,128)(2,1)S(1)}, bf16[96,1536]{1,0:T(8,128)(2,1)S(1)}, u32[]{:S(2)}, u32[]{:S(2)}) %collective-permute-start.30) | collective-permute-done | bytes 294944 | tf_op jit(solution)/shard_map/ppermute | solution.py:84
  443.3 5.7 %collective-permute-done.40 = bf16[192,768]{1,0:T(8,128)(2,1)S(1)} collective-permute-done((bf16[192,768]{1,0:T(8,128)(2,1)S(1)}, bf16[192,768]{1,0:T(8,128)(2,1)S(1)}, u32[]{:S(2)}, u32[]{:S(2)}) %collective-permute-start.40) | collective-permute-done | bytes 294944 | tf_op jit(solution)/shard_map/ppermute | solution.py:84
  455.6 22.4 %collective-permute-done.41 = bf16[384,768]{1,0:T(8,128)(2,1)S(1)} collective-permute-done((bf16[384,768]{1,0:T(8,128)(2,1)S(1)}, bf16[384,768]{1,0:T(8,128)(2,1)S(1)}, u32[]{:S(2)}, u32[]{:S(2)}) %collective-permute-start.41) | collective-permute-done | bytes 589856 | tf_op jit(solution)/shard_map/ppermute | solution.py:84
  482.6 6.3 %collective-permute-done.61 = bf16[384,768]{1,0:T(8,128)(2,1)S(1)} collective-permute-done((bf16[384,768]{1,0:T(8,128)(2,1)S(1)}, bf16[384,768]{1,0:T(8,128)(2,1)S(1)}, u32[]{:S(2)}, u32[]{:S(2)}) %collective-permute-start.61) | collective-permute-done | bytes 589856 | tf_op jit(solution)/shard_map/ppermute | solution.py:84
  (419 shorter events, 211.4 us)
Async XLA Ops:
  4.7 81.0 %collective-permute-start.12 = (bf16[384,768]{1,0:T(8,128)(2,1)}, bf16[384,768]{1,0:T(8,128)(2,1)}, u32[]{:S(2)}, u32[]{:S(2)}) collective-permute-start(bf16[384,768]{1,0:T(8,128)(2,1)} %constant_dynamic-slice_fusion.20), channel_id=1, source_target_pairs={{0,1},{1,0},{2,3},{3,2},{4,5},{5,4},{6,7},{7,6},{8,9},{9,8},{10,11... | collective-permute-start | bytes 1769480 | tf_op jit(solution)/shard_map/ppermute | solution.py:88
  8.7 61.5 %collective-permute-start.5 = (bf16[384,768]{1,0:T(8,128)(2,1)}, bf16[384,768]{1,0:T(8,128)(2,1)}, u32[]{:S(2)}, u32[]{:S(2)}) collective-permute-start(bf16[384,768]{1,0:T(8,128)(2,1)} %constant_dynamic-slice_fusion.22), channel_id=1, source_target_pairs={{0,1},{1,0},{2,3},{3,2},{4,5},{5,4},{6,7},{7,6},{8,9},{9,8},{10,11... | collective-permute-start | bytes 1769480 | tf_op jit(solution)/shard_map/ppermute | solution.py:88
  21.5 66.2 %collective-permute-start.8 = (bf16[192,1536]{1,0:T(8,128)(2,1)}, bf16[192,1536]{1,0:T(8,128)(2,1)S(1)}, u32[]{:S(2)}, u32[]{:S(2)}) collective-permute-start(bf16[192,1536]{1,0:T(8,128)(2,1)} %constant_dynamic-slice_fusion.21), channel_id=1, source_target_pairs={{0,1},{1,0},{2,3},{3,2},{4,5},{5,4},{6,7},{7,6},{8,9},{9,8},{10,11... | collective-permute-start | bytes 1769480 | tf_op jit(solution)/shard_map/ppermute | solution.py:88
  21.6 45.9 %collective-permute-start.1 = (bf16[192,1536]{1,0:T(8,128)(2,1)S(1)}, bf16[192,1536]{1,0:T(8,128)(2,1)S(1)}, u32[]{:S(2)}, u32[]{:S(2)}) collective-permute-start(bf16[192,1536]{1,0:T(8,128)(2,1)S(1)} %constant_dynamic-slice_fusion.23), channel_id=1, source_target_pairs={{0,1},{1,0},{2,3},{3,2},{4,5},{5,4},{6,7},{7,6},{8,9},{9,8},{10,11... | collective-permute-start | bytes 1769480 | tf_op jit(solution)/shard_map/ppermute | solution.py:88
  42.4 96.6 %collective-permute-start.16 = (bf16[256,768]{1,0:T(8,128)(2,1)}, bf16[256,768]{1,0:T(8,128)(2,1)S(1)}, u32[]{:S(2)}, u32[]{:S(2)}) collective-permute-start(bf16[256,768]{1,0:T(8,128)(2,1)} %get-tuple-element.47), channel_id=1, source_target_pairs={{0,1},{1,0},{2,3},{3,2},{4,5},{5,4},{6,7},{7,6},{8,9},{9,8},{10,11... | collective-permute-start | bytes 1179656 | tf_op jit(solution)/shard_map/ppermute | solution.py:88
  84.2 36.5 %collective-permute-start.3 = (bf16[384,1536]{1,0:T(8,128)(2,1)S(1)}, bf16[384,1536]{1,0:T(8,128)(2,1)S(1)}, u32[]{:S(2)}, u32[]{:S(2)}) collective-permute-start(bf16[384,1536]{1,0:T(8,128)(2,1)S(1)} %maximum_select_fusion.8), channel_id=1, source_target_pairs={{0,2},{2,0},{4,6},{6,4},{8,10},{10,8},{12,14},{14,12},{16,18},{18,... | collective-permute-start | bytes 3538952 | tf_op jit(solution)/shard_map/ppermute | solution.py:84
  196.7 47.2 %collective-permute-start.54 = (bf16[768,768]{1,0:T(8,128)(2,1)}, bf16[768,768]{1,0:T(8,128)(2,1)}, u32[]{:S(2)}, u32[]{:S(2)}) collective-permute-start(bf16[768,768]{1,0:T(8,128)(2,1)} %constant_dynamic-slice_fusion.3), channel_id=1, source_target_pairs={{0,2},{2,0},{4,6},{6,4},{8,10},{10,8},{12,14},{14,12},{16,18},{18,... | collective-permute-start | bytes 3538952 | tf_op jit(solution)/shard_map/ppermute | solution.py:84
  199.9 46.3 %collective-permute-start.44 = (bf16[384,1536]{1,0:T(8,128)(2,1)}, bf16[384,1536]{1,0:T(8,128)(2,1)}, u32[]{:S(2)}, u32[]{:S(2)}) collective-permute-start(bf16[384,1536]{1,0:T(8,128)(2,1)} %constant_dynamic-slice_fusion.8), channel_id=1, source_target_pairs={{0,2},{2,0},{4,6},{6,4},{8,10},{10,8},{12,14},{14,12},{16,18},{18,... | collective-permute-start | bytes 3538952 | tf_op jit(solution)/shard_map/ppermute | solution.py:84
  201.0 48.3 %collective-permute-start.34 = (bf16[768,768]{1,0:T(8,128)(2,1)}, bf16[768,768]{1,0:T(8,128)(2,1)}, u32[]{:S(2)}, u32[]{:S(2)}) collective-permute-start(bf16[768,768]{1,0:T(8,128)(2,1)} %constant_dynamic-slice_fusion.13), channel_id=1, source_target_pairs={{0,2},{2,0},{4,6},{6,4},{8,10},{10,8},{12,14},{14,12},{16,18},{18,... | collective-permute-start | bytes 3538952 | tf_op jit(solution)/shard_map/ppermute | solution.py:84
  243.9 33.2 %collective-permute-start.43 = (bf16[384,1536]{1,0:T(8,128)(2,1)S(1)}, bf16[384,1536]{1,0:T(8,128)(2,1)S(1)}, u32[]{:S(2)}, u32[]{:S(2)}) collective-permute-start(bf16[384,1536]{1,0:T(8,128)(2,1)S(1)} %copy-done.19), channel_id=1, source_target_pairs={{0,2},{2,0},{4,6},{6,4},{8,10},{10,8},{12,14},{14,12},{16,18},{18,... | collective-permute-start | bytes 3538952 | tf_op jit(solution)/shard_map/ppermute | solution.py:84
  249.3 51.1 %collective-permute-start.45 = (bf16[384,1536]{1,0:T(8,128)(2,1)S(1)}, bf16[384,1536]{1,0:T(8,128)(2,1)S(1)}, u32[]{:S(2)}, u32[]{:S(2)}) collective-permute-start(bf16[384,1536]{1,0:T(8,128)(2,1)S(1)} %add_convert_fusion.8), channel_id=1, source_target_pairs={{0,1},{1,0},{2,3},{3,2},{4,5},{5,4},{6,7},{7,6},{8,9},{9,8},{10,11... | collective-permute-start | bytes 3538952 | tf_op jit(solution)/shard_map/ppermute | solution.py:88
  251.6 50.7 %collective-permute-start.33 = (bf16[768,768]{1,0:T(8,128)(2,1)S(1)}, bf16[768,768]{1,0:T(8,128)(2,1)S(1)}, u32[]{:S(2)}, u32[]{:S(2)}) collective-permute-start(bf16[768,768]{1,0:T(8,128)(2,1)S(1)} %constant_dynamic-slice_fusion.14), channel_id=1, source_target_pairs={{0,2},{2,0},{4,6},{6,4},{8,10},{10,8},{12,14},{14,12},{16,18},{18,... | collective-permute-start | bytes 3538952 | tf_op jit(solution)/shard_map/ppermute | solution.py:84
  252.0 75.8 %collective-permute-start.23 = (bf16[384,1536]{1,0:T(8,128)(2,1)S(1)}, bf16[384,1536]{1,0:T(8,128)(2,1)S(1)}, u32[]{:S(2)}, u32[]{:S(2)}) collective-permute-start(bf16[384,1536]{1,0:T(8,128)(2,1)S(1)} %constant_dynamic-slice_fusion.19), channel_id=1, source_target_pairs={{0,2},{2,0},{4,6},{6,4},{8,10},{10,8},{12,14},{14,12},{16,18},{18,... | collective-permute-start | bytes 3538952 | tf_op jit(solution)/shard_map/ppermute | solution.py:84
  275.1 50.6 %collective-permute-start.35 = (bf16[768,768]{1,0:T(8,128)(2,1)S(1)}, bf16[768,768]{1,0:T(8,128)(2,1)S(1)}, u32[]{:S(2)}, u32[]{:S(2)}) collective-permute-start(bf16[768,768]{1,0:T(8,128)(2,1)S(1)} %add_convert_fusion.11), channel_id=1, source_target_pairs={{0,1},{1,0},{2,3},{3,2},{4,5},{5,4},{6,7},{7,6},{8,9},{9,8},{10,11... | collective-permute-start | bytes 3538952 | tf_op jit(solution)/shard_map/ppermute | solution.py:88
  277.1 203.9 %collective-permute-start.17 = (bf16[256,768]{1,0:T(8,128)(2,1)S(1)}, bf16[256,768]{1,0:T(8,128)(2,1)S(1)}, u32[]{:S(2)}, u32[]{:S(2)}) collective-permute-start(bf16[256,768]{1,0:T(8,128)(2,1)S(1)} %get-tuple-element.45), channel_id=1, source_target_pairs={{0,1},{1,0},{2,3},{3,2},{4,5},{5,4},{6,7},{7,6},{8,9},{9,8},{10,11... | collective-permute-start | bytes 1179656 | tf_op jit(solution)/shard_map/ppermute | solution.py:88
  300.4 58.1 %collective-permute-start.25 = (bf16[384,1536]{1,0:T(8,128)(2,1)S(1)}, bf16[384,1536]{1,0:T(8,128)(2,1)S(1)}, u32[]{:S(2)}, u32[]{:S(2)}) collective-permute-start(bf16[384,1536]{1,0:T(8,128)(2,1)S(1)} %add_convert_fusion.14), channel_id=1, source_target_pairs={{0,1},{1,0},{2,3},{3,2},{4,5},{5,4},{6,7},{7,6},{8,9},{9,8},{10,11... | collective-permute-start | bytes 3538952 | tf_op jit(solution)/shard_map/ppermute | solution.py:88
  302.3 58.3 %collective-permute-start.56 = (bf16[384,768]{1,0:T(8,128)(2,1)S(1)}, bf16[384,768]{1,0:T(8,128)(2,1)S(1)}, u32[]{:S(2)}, u32[]{:S(2)}) collective-permute-start(bf16[384,768]{1,0:T(8,128)(2,1)S(1)} %constant_dynamic-slice_fusion.2), channel_id=1, source_target_pairs={{0,4},{2,6},{4,0},{6,2},{8,12},{10,14},{12,8},{14,10},{16,20},{18,... | collective-permute-start | bytes 1769480 | tf_op jit(solution)/shard_map/ppermute | solution.py:84
  325.7 36.8 %collective-permute-start.46 = (bf16[192,1536]{1,0:T(8,128)(2,1)S(1)}, bf16[192,1536]{1,0:T(8,128)(2,1)S(1)}, u32[]{:S(2)}, u32[]{:S(2)}) collective-permute-start(bf16[192,1536]{1,0:T(8,128)(2,1)S(1)} %constant_dynamic-slice_fusion.7), channel_id=1, source_target_pairs={{0,4},{2,6},{4,0},{6,2},{8,12},{10,14},{12,8},{14,10},{16,20},{18,... | collective-permute-start | bytes 1769480 | tf_op jit(solution)/shard_map/ppermute | solution.py:84
  327.8 35.4 %collective-permute-start.36 = (bf16[384,768]{1,0:T(8,128)(2,1)S(1)}, bf16[384,768]{1,0:T(8,128)(2,1)S(1)}, u32[]{:S(2)}, u32[]{:S(2)}) collective-permute-start(bf16[384,768]{1,0:T(8,128)(2,1)S(1)} %constant_dynamic-slice_fusion.12), channel_id=1, source_target_pairs={{0,4},{2,6},{4,0},{6,2},{8,12},{10,14},{12,8},{14,10},{16,20},{18,... | collective-permute-start | bytes 1769480 | tf_op jit(solution)/shard_map/ppermute | solution.py:84
  378.8 33.4 %collective-permute-start.48 = (bf16[48,1536]{1,0:T(8,128)(2,1)S(1)}, bf16[48,1536]{1,0:T(8,128)(2,1)S(1)}, u32[]{:S(2)}, u32[]{:S(2)}) collective-permute-start(bf16[48,1536]{1,0:T(8,128)(2,1)S(1)} %constant_dynamic-slice_fusion.5), channel_id=1, source_target_pairs={{0,16},{2,18},{4,20},{6,22},{8,24},{10,26},{12,28},{14,30},{16,0},... | collective-permute-start | bytes 442376 | tf_op jit(solution)/shard_map/ppermute | solution.py:84
  396.2 42.7 %collective-permute-start.59 = (bf16[96,768]{1,0:T(8,128)(2,1)S(1)}, bf16[96,768]{1,0:T(8,128)(2,1)S(1)}, u32[]{:S(2)}, u32[]{:S(2)}) collective-permute-start(bf16[96,768]{1,0:T(8,128)(2,1)S(1)} %add_convert_fusion.24), channel_id=1, source_target_pairs={{0,16},{2,18},{4,20},{6,22},{8,24},{10,26},{12,28},{14,30},{16,0},... | collective-permute-start | bytes 442376 | tf_op jit(solution)/shard_map/ppermute | solution.py:84
  442.7 36.5 %collective-permute-start.51 = (bf16[192,1536]{1,0:T(8,128)(2,1)S(1)}, bf16[192,1536]{1,0:T(8,128)(2,1)S(1)}, u32[]{:S(2)}, u32[]{:S(2)}) collective-permute-start(bf16[192,1536]{1,0:T(8,128)(2,1)S(1)} %maximum_select_fusion.20), channel_id=1, source_target_pairs={{0,4},{2,6},{4,0},{6,2},{8,12},{10,14},{12,8},{14,10},{16,20},{18,... | collective-permute-start | bytes 1769480 | tf_op jit(solution)/shard_map/ppermute | solution.py:84
  453.1 38.6 %collective-permute-start.32 = (bf16[384,1536]{1,0:T(8,128)(2,1)S(1)}, bf16[384,1536]{1,0:T(8,128)(2,1)S(1)}, u32[]{:S(2)}, u32[]{:S(2)}) collective-permute-start(bf16[384,1536]{1,0:T(8,128)(2,1)S(1)} %maximum_select_fusion.12), channel_id=1, source_target_pairs={{0,2},{2,0},{4,6},{6,4},{8,10},{10,8},{12,14},{14,12},{16,18},{18,... | collective-permute-start | bytes 3538952 | tf_op jit(solution)/shard_map/ppermute | solution.py:84
  455.0 33.8 %collective-permute-start.61 = (bf16[384,768]{1,0:T(8,128)(2,1)S(1)}, bf16[384,768]{1,0:T(8,128)(2,1)S(1)}, u32[]{:S(2)}, u32[]{:S(2)}) collective-permute-start(bf16[384,768]{1,0:T(8,128)(2,1)S(1)} %maximum_select_fusion.21), channel_id=1, source_target_pairs={{0,4},{2,6},{4,0},{6,2},{8,12},{10,14},{12,8},{14,10},{16,20},{18,... | collective-permute-start | bytes 1769480 | tf_op jit(solution)/shard_map/ppermute | solution.py:84
  (114 other events, 1457.2 us)

commit v2 on v1

v2 whole, which is shorter than its diff:
```python
import math

import jax
import jax.numpy as jnp
import numpy as np
from jax import lax
from jax.experimental import pallas as pl
from jax.sharding import PartitionSpec as P

norm_eps = 1e-05
low_type = jnp.bfloat16
wide_type = jnp.float32


def fourier_table(points):
    indices = np.arange(points, dtype=np.int64)
    phases = (indices[:, None] * indices[None, :]) % points
    angles = phases.astype(np.float32) * np.float32(2.0 * math.pi / points)
    factor = np.float32(points ** (-0.5))
    return (np.cos(angles) * factor, np.sin(angles) * factor)


def dot(left, right):
    return jnp.dot(left, right, preferred_element_type=wide_type)


def dot_tn(left, right):
    return lax.dot_general(left, right, (((0,), (0,)), ((), ())), preferred_element_type=wide_type)


def dot_nt(left, right):
    return lax.dot_general(left, right, (((1,), (1,)), ((), ())), preferred_element_type=wide_type)


def normalize(activity):
    center = jnp.mean(activity, axis=-1, keepdims=True)
    centered = activity - center
    spread = jnp.mean(centered * centered, axis=-1, keepdims=True)
    inverse = lax.rsqrt(spread + norm_eps)
    return centered * inverse, inverse


def norm_backward(grad, normal, inverse, gain):
    pulled = grad * gain
    first = jnp.mean(pulled, axis=-1, keepdims=True)
    second = jnp.mean(pulled * normal, axis=-1, keepdims=True)
    return inverse * (pulled - first - normal * second)


def gate_pair(preact):
    scale = math.sqrt(2.0 / math.pi)
    square = preact * preact
    turn = jnp.tanh(scale * (preact + 0.044715 * preact * square))
    half = 0.5 * (1.0 + turn)
    slope = half + (0.5 * scale) * preact * (1.0 - turn * turn) * (1.0 + 3 * 0.044715 * square)
    return (preact * half).astype(low_type), slope.astype(low_type)


def flip_pairs(size, bit):
    return [(index, index ^ bit) for index in range(size)]


def order_halves(bit_value, mine, theirs, axis=0):
    return jnp.where(
        bit_value == 0,
        jnp.concatenate([mine, theirs], axis=axis),
        jnp.concatenate([theirs, mine], axis=axis),
    )


def take_block(array, which, count=2, axis=0):
    size = array.shape[axis] // count
    return lax.dynamic_slice_in_dim(array, which * size, size, axis)


def dp_bits():
    return [1 << level for level in range(lax.axis_size("dp").bit_length() - 1)]


def bit_of(bit):
    return (lax.axis_index("dp") // bit) % 2


def dp_swap(array, bit):
    return lax.ppermute(array, "dp", flip_pairs(lax.axis_size("dp"), bit))


def mp_swap(array):
    return lax.ppermute(array, "mp", [(0, 1), (1, 0)])


def add_low(left, right):
    return (left.astype(wide_type) + right.astype(wide_type)).astype(low_type)


def gate(value, *earlier):
    def kernel(*refs):
        pass

    anywhere = pl.BlockSpec(memory_space=pl.ANY)
    return pl.pallas_call(
        kernel,
        out_shape=jax.ShapeDtypeStruct(value.shape, value.dtype),
        in_specs=[anywhere] * (1 + len(earlier)),
        out_specs=anywhere,
        input_output_aliases={0: 0},
        name="gate",
    )(value, *earlier)


def fetch_pieces(weight, bits):
    piece = weight
    for bit in bits:
        piece = take_block(piece, bit_of(bit))
    return piece


def fetch_join(piece, bit):
    return order_halves(bit_of(bit), piece, dp_swap(piece, bit))


def far_piece(up_weight, down_weight):
    core = dp_bits()[0]
    place, count = lax.axis_index("dp") // 2, lax.axis_size("dp") // 2
    return jnp.concatenate(
        [
            take_block(take_block(up_weight, bit_of(core), axis=1), place, count),
            take_block(take_block(down_weight, bit_of(core)), place, count),
        ]
    )


def far_weights(pieces):
    half = pieces.shape[1] // 2
    width = pieces.shape[2]
    return pieces[:, :half].reshape(-1, width), pieces[:, half:].reshape(-1, width)


def core_groups():
    return [
        [place for place in range(lax.axis_size("dp")) if place % 2 == which] for which in (0, 1)
    ]


def total_plain(part, hidden_axis):
    own = lax.psum_scatter(part, "mp", scatter_dimension=hidden_axis, tiled=True)
    return lax.psum(own, "dp").astype(wide_type)


def total_small(vector):
    for bit in dp_bits():
        vector = vector + dp_swap(vector, bit)
    if lax.axis_size("mp") == 2:
        return vector + mp_swap(vector)
    return lax.psum(vector, "mp")


def given_row(array):
    return lax.dynamic_index_in_dim(array, 1 - lax.axis_index("mp"), 0, keepdims=False)


def joined_row(array, received):
    own = lax.dynamic_index_in_dim(array, lax.axis_index("mp"), 0, keepdims=False)
    return jnp.concatenate([own, received], axis=0)


def gathered_row(array):
    return lax.all_to_all(array, "mp", split_axis=0, concat_axis=1, tiled=True)[0]


def return_rows(array):
    if lax.axis_size("mp") == 2:
        half = array.shape[0] // 2
        own, received = array[None, :half], mp_swap(array[None, half:])
        return order_halves(lax.axis_index("mp"), own, received)
    return lax.all_to_all(array[None], "mp", split_axis=1, concat_axis=0, tiled=True)


def layer_mix(layer_in, live_mask, params, tables, *earlier):
    gain_mix, shift_mix = params[:2]
    pair_table, wide_table, stack_table = tables
    width = layer_in.shape[1]
    masked = layer_in * live_mask
    spectra = dot(masked.astype(low_type), wide_table).astype(low_type)
    if earlier:
        spectra = gate(spectra, *earlier)
    stacked = jnp.concatenate([spectra[:, :width], spectra[:, width:]], axis=0)
    summed = masked + dot(pair_table, stacked)
    normal, inverse = normalize(summed)
    normed = normal * gain_mix + shift_mix
    return summed, normed, normed.astype(low_type)


def layer_hidden(normed_low, up_weight, up_bias):
    return gate_pair(dot(normed_low, up_weight) + up_bias.astype(wide_type))


def layer_out(normed, branch, live_mask, params):
    down_bias, gain_out, shift_out = params[2:]
    residual = normed + branch + down_bias
    out_normal, out_inverse = normalize(residual)
    result = (out_normal * gain_out + shift_out) * live_mask
    return result, residual


def out_backward(result_cot, live_mask, gain_out, residual):
    out_grad = result_cot * live_mask
    out_normal, out_inverse = normalize(residual)
    resid_grad = norm_backward(out_grad, out_normal, out_inverse, gain_out)
    gainout_grad = jnp.sum(out_grad * out_normal, axis=0)
    shiftout_grad = jnp.sum(out_grad, axis=0)
    branch_cot = resid_grad.astype(low_type)
    downbias_grad = jnp.sum(branch_cot, axis=0, dtype=wide_type)
    return resid_grad, branch_cot, (downbias_grad, gainout_grad, shiftout_grad)


def cot_of(branch_cot, down_weight, slope):
    return (dot_nt(branch_cot, down_weight) * slope.astype(wide_type)).astype(low_type)


def mix_backward(normed_grad, live_mask, gain_mix, summed, tables):
    pair_table, wide_table, stack_table = tables
    length = summed.shape[0]
    normal, inverse = normalize(summed)
    summed_grad = norm_backward(normed_grad, normal, inverse, gain_mix)
    gainmix_grad = jnp.sum(normed_grad * normal, axis=0)
    shiftmix_grad = jnp.sum(normed_grad, axis=0)
    summed_low = summed_grad.astype(low_type)
    flat_grad = jnp.concatenate(
        [
            dot(pair_table[:, :length], summed_low).astype(low_type),
            dot(pair_table[:, length:], summed_low).astype(low_type),
        ],
        axis=1,
    )
    masked_grad = (summed_grad + dot(flat_grad, stack_table)) * live_mask
    return masked_grad, (gainmix_grad, shiftmix_grad)


def paired(first, second):
    return dot_tn(*first) + dot_tn(*second)


def core_swap(array):
    return dp_swap(array, dp_bits()[0])


def shared_forward(normed_low, weights, biases):
    normed_near = core_swap(normed_low)
    kept = []
    for (up_weight, down_weight), bias in zip(weights, biases):
        kept.append(
            (
                layer_hidden(normed_low, up_weight, bias),
                layer_hidden(normed_near, up_weight, bias),
            )
        )
    near_branch = sum(
        dot(near[0], down_weight) for (_, near), (_, down_weight) in zip(kept, weights)
    )
    received = core_swap(near_branch.astype(low_type))
    branch = sum(dot(own[0], down_weight) for (own, _), (_, down_weight) in zip(kept, weights))
    return branch + received.astype(wide_type), normed_near, kept


def far_shape(array):
    bits = len(dp_bits()) - 1
    return array.reshape((2,) * bits + (-1, array.shape[-1]))


def far_scatter(total):
    total = far_shape(total)
    bits = dp_bits()[1:]
    for level, bit in enumerate(bits):
        axis = len(bits) - 1 - level
        which = bit_of(bit)
        given = lax.dynamic_index_in_dim(total, 1 - which, axis, False)
        own = lax.dynamic_index_in_dim(total, which, axis, False)
        total = add_low(own, dp_swap(given, bit))
    return total


def far_gather(piece):
    bits = dp_bits()[1:]
    total = piece
    for level, bit in list(enumerate(bits))[::-1]:
        theirs = dp_swap(total, bit)
        axis = len(bits) - 1 - level
        total = order_halves(
            bit_of(bit), jnp.expand_dims(total, axis), jnp.expand_dims(theirs, axis), axis
        )
    return total.reshape(-1, piece.shape[-1])


def shared_backward(resid_grad, branch_cot, normed_pair, weights, kept, *earlier):
    normed_low, normed_near = normed_pair
    cot_near = core_swap(branch_cot)
    downs, ups, bias = [None] * 2, [None] * 2, [None] * 2
    own_cots, near_cots = [None] * 2, [None] * 2
    for step in (1, 0):
        (hidden, slope), (hidden_near, slope_near) = kept[step]
        downs[step] = paired((hidden, branch_cot), (hidden_near, cot_near)).astype(low_type)
        down_weight = weights[step][1]
        own_cots[step] = cot_of(branch_cot, down_weight, slope)
        near_cots[step] = cot_of(cot_near, down_weight, slope_near)
        bias[step] = jnp.sum(own_cots[step], axis=0, dtype=wide_type) + jnp.sum(
            near_cots[step], axis=0, dtype=wide_type
        )
    for step in (1, 0):
        ups[step] = paired(
            (normed_low, own_cots[step]), (normed_near, near_cots[step])
        ).astype(low_type)
    near_grad = sum(dot_nt(cot, weight[0]) for cot, weight in zip(near_cots, weights))
    near_grad = near_grad.astype(low_type)
    if earlier:
        near_grad = gate(near_grad, *earlier)
    received = core_swap(near_grad)
    normed_grad = resid_grad + sum(dot_nt(cot, weight[0]) for cot, weight in zip(own_cots, weights))
    return normed_grad + received.astype(wide_type), downs, ups, bias


def backward_overlapped(grad, live_mask, params, weights, tables, saved):
    bits = dp_bits()
    core = bit_of(bits[0])
    gain_mix, _, _, gain_out, _ = params[1]
    summed, normed_pair, residual, kept = saved[1]
    width = summed.shape[1]
    resid_grad, branch_cot, small_out = out_backward(grad, live_mask, gain_out, residual)
    normed_grad, downs_two, ups_two, bias_two = shared_backward(
        resid_grad, branch_cot, normed_pair, weights[1], kept
    )
    scattered = lax.psum_scatter(
        jnp.concatenate(
            [
                downs_two[0].reshape(lax.axis_size("dp") // 2, -1, width),
                downs_two[1].reshape(lax.axis_size("dp") // 2, -1, width),
            ],
            axis=1,
        ),
        "dp",
        scatter_dimension=0,
        axis_index_groups=core_groups(),
        tiled=False,
    )
    up_two_other = mp_swap(ups_two[1])
    grad, small_mix = mix_backward(normed_grad, live_mask, gain_mix, summed, tables)
    small_two = small_mix + small_out
    gain_mix, _, _, gain_out, _ = params[0]
    summed, normed_pair, residual, kept = saved[0]
    resid_grad, branch_cot, small_out = out_backward(grad, live_mask, gain_out, residual)
    up_two = add_low(ups_two[0], up_two_other)
    normed_grad, downs_one, ups_one, bias_one = shared_backward(
        resid_grad, branch_cot, normed_pair, weights[0], kept, up_two
    )
    down_one_other = mp_swap(gate(downs_one[1], up_two))
    grad, small_mix = mix_backward(normed_grad, live_mask, gain_mix, summed, tables)
    small_one = small_mix + small_out
    up_two_piece = far_scatter(up_two)
    half = scattered.shape[0] // 2
    down_two_piece = add_low(scattered[:half], mp_swap(scattered[half:]))
    both = lax.all_gather(
        jnp.concatenate([up_two_piece, down_two_piece], axis=0), "dp", axis=0, tiled=False
    )
    down_one = add_low(downs_one[0], down_one_other)
    up_one_other = mp_swap(gate(ups_one[1], down_one))
    down_one = far_gather(far_scatter(down_one))
    up_one = add_low(ups_one[0], up_one_other)
    up_one = far_gather(far_scatter(up_one))
    up_one = order_halves(core, up_one, core_swap(up_one), 1).astype(wide_type)
    down_one = order_halves(core, down_one, core_swap(down_one), 0).astype(wide_type)
    both = both.reshape(lax.axis_size("dp") // 2, 2, 2, -1, width)
    up_two = both[:, :, 0].transpose(0, 2, 1, 3).reshape(-1, 2 * width).astype(wide_type)
    down_two = both[:, :, 1].transpose(1, 0, 2, 3).reshape(-1, width).astype(wide_type)
    large = ((up_one, down_one), (up_two, down_two))
    return grad, large, (small_one, small_two), (bias_one, bias_two)


def backward_plain(grad, live_mask, params, weights, tables, saved):
    large, small, bias = [None] * 2, [None] * 2, [None] * 2
    for level in (1, 0):
        gain_mix, _, _, gain_out, _ = params[level]
        summed, normed_low, residual, kept = saved[level]
        ((up_weight, down_weight),) = weights[level]
        ((hidden, slope),) = kept
        resid_grad, branch_cot, small_out = out_backward(grad, live_mask, gain_out, residual)
        down_grad = dot_tn(hidden, branch_cot).astype(low_type)
        cot = cot_of(branch_cot, down_weight, slope)
        up_grad = dot_tn(normed_low, cot).astype(low_type)
        bias[level] = [jnp.sum(cot, axis=0, dtype=wide_type)]
        grad, small_mix = mix_backward(
            resid_grad + dot_nt(cot, up_weight), live_mask, gain_mix, summed, tables
        )
        small[level] = small_mix + small_out
        large[level] = (total_plain(up_grad, 1), total_plain(down_grad, 0))
    return grad, large, small, bias


def whole_bias(parts):
    if len(parts) == 1:
        return parts[0]
    core, mine = bit_of(dp_bits()[0]), lax.axis_index("mp")
    index = jnp.arange(4, dtype=jnp.int32)[:, None]
    own = jnp.where(index == 2 * mine + core, parts[0][None], 0.0)
    other = jnp.where(index == 2 * (1 - mine) + core, parts[1][None], 0.0)
    return (own + other).reshape(-1)


def on_device(*arguments):
    inputs, pad_counts = arguments[:2]
    layer_args = (arguments[2:10], arguments[10:18])
    cotangent = arguments[18]
    mp_count = lax.axis_size("mp")
    mine = lax.axis_index("mp")
    feature_width = inputs.shape[2]
    row_length = inputs.shape[1] * mp_count
    cos_seq, sin_seq = fourier_table(row_length)
    pair_full = np.concatenate([cos_seq, -sin_seq], axis=1)
    turned = 1 - 2 * ((np.arange(row_length)[:, None] + np.arange(2 * row_length)[None, :]) % 2)
    position = jnp.arange(row_length, dtype=jnp.int32)
    if mp_count == 2:
        pair_table = lax.dynamic_index_in_dim(
            jnp.asarray(np.stack([pair_full, pair_full * turned]), low_type), mine, 0, False
        )
        position = (position + mine * inputs.shape[1]) % row_length
    else:
        pair_table = jnp.asarray(pair_full, low_type)
    wide_table = jnp.asarray(np.concatenate(fourier_table(feature_width), axis=1), low_type)
    stack_table = jnp.asarray(np.concatenate(fourier_table(feature_width), axis=0), low_type)
    tables = (pair_table, wide_table, stack_table)
    pads = lax.dynamic_index_in_dim(pad_counts, mine, 0, False)
    live_mask = (position < row_length - pads).astype(wide_type)[:, None]
    vectors = jnp.stack(
        [member for args in layer_args for member in (args[0], args[1], args[5], args[6], args[7])]
    )
    if mp_count == 2:
        vectors = gate(vectors)
    vectors = vectors.astype(wide_type)
    params = [tuple(vectors[5 * level + step] for step in range(5)) for level in range(2)]
    (up_one, down_one), (up_two, down_two) = [(args[2], args[4]) for args in layer_args]
    biases = jnp.stack([args[3] for args in layer_args])
    saved = []
    if mp_count == 2:
        core, near, far = dp_bits()[:3]
        core_bit = bit_of(core)
        there = lambda array, bits, axis: fetch_pieces(take_block(array, core_bit, axis=axis), bits)
        far_part = mp_swap(far_piece(up_two, down_two))
        received = mp_swap(given_row(inputs))
        up_part = mp_swap(there(up_one, (near, far), 1))
        other_biases = mp_swap(biases)
        down_part = mp_swap(gate(there(down_one, (far, near), 0), received))
        received_cot = mp_swap(gate(given_row(cotangent), down_part))
        far_parts = lax.all_gather(
            far_part, "dp", axis=0, tiled=False, axis_index_groups=core_groups()
        )
        biases = [
            [take_block(array, core_bit, axis=1)[level] for array in (biases, other_biases)]
            for level in range(2)
        ]
        row_in = joined_row(inputs, received).astype(wide_type)
        up_part = fetch_join(up_part, far)
        summed, normed, normed_low = layer_mix(row_in, live_mask, params[0], tables, up_part)
        down_part = fetch_join(down_part, near)
        up_part = fetch_join(up_part, near)
        down_part = fetch_join(down_part, far)
        own_blocks = lambda up, down: (take_block(up, core_bit, axis=1), take_block(down, core_bit))
        weights = [
            (own_blocks(up_one, down_one), (up_part, down_part)),
            (own_blocks(up_two, down_two), far_weights(far_parts)),
        ]
        current = row_in
        for level in range(2):
            if level:
                summed, normed, normed_low = layer_mix(current, live_mask, params[1], tables)
            branch, normed_near, kept = shared_forward(normed_low, weights[level], biases[level])
            current, residual = layer_out(normed, branch, live_mask, params[level])
            saved.append((summed, (normed_low, normed_near), residual, kept))
        row_cot = joined_row(cotangent, received_cot)
    else:
        weights = []
        biases = lax.all_gather(biases, "mp", axis=1, tiled=True)
        current = gathered_row(inputs).astype(wide_type)
        for level, (up_weight, down_weight) in enumerate(((up_one, down_one), (up_two, down_two))):
            up_weight = lax.all_gather(up_weight, "mp", axis=1, tiled=True)
            down_weight = lax.all_gather(down_weight, "mp", axis=0, tiled=True)
            weights.append(((up_weight, down_weight),))
            summed, normed, normed_low = layer_mix(current, live_mask, params[level], tables)
            kept = layer_hidden(normed_low, up_weight, biases[level])
            current, residual = layer_out(
                normed, dot(kept[0], down_weight), live_mask, params[level]
            )
            saved.append((summed, normed_low, residual, (kept,)))
        row_cot = gathered_row(cotangent)
    final_out = return_rows(current.astype(low_type))
    backward = backward_overlapped if mp_count == 2 else backward_plain
    grad, large, small, bias = backward(
        row_cot.astype(wide_type), live_mask, params, weights, tables, saved
    )
    input_grad = return_rows(grad.astype(low_type)).astype(wide_type)
    hidden_own = layer_args[0][3].shape[0]
    pieces = []
    for level in range(2):
        pieces.extend(small[level])
        pieces.append(whole_bias(bias[level]))
    vector = total_small(jnp.concatenate(pieces))
    results = [final_out, input_grad]
    offset = 0
    for level in range(2):
        vectors = []
        for _ in range(5):
            vectors.append(vector[offset : offset + feature_width])
            offset += feature_width
        bias_total = lax.dynamic_slice_in_dim(
            vector, offset + mine * hidden_own, hidden_own, 0
        )
        offset += hidden_own * mp_count
        gainmix, shiftmix, downbias, gainout, shiftout = vectors
        up_total, down_total = large[level]
        results += [gainmix, shiftmix, up_total, bias_total, down_total, downbias, gainout, shiftout]
    return tuple(results)


def solution(mesh):
    layer_specs = (P(), P(), P(None, "mp"), P("mp"), P("mp", None), P(), P(), P())
    rows = P("dp", "mp", None)
    return jax.shard_map(
        on_device,
        mesh=mesh,
        in_specs=(rows, P("dp"), *layer_specs, *layer_specs, rows),
        out_specs=(rows, rows, *layer_specs, *layer_specs),
        check_vma=False,
    )
```

time: 511 us -> 429 us (0.84)
  waiting for transfers between devices: 275 us -> 102 us
  local copies, waits for them, and re-layouts: 26.7 us -> 67.8 us
  matrix products: 91.1 us -> 130 us
  starting transfers between devices: 66.7 us -> 42.2 us
  other arithmetic: 40.3 us -> 63.9 us
  between operations: 3.53 us -> 16.5 us
    ppermute x15 -> x13, waiting for transfers between devices: 136 us -> 17.5 us  [mp_swap(): return lax.ppermute(array, 'mp', [(0, 1), (1, 0)])]
    ppermute x48 -> x33, waiting for transfers between devices: 139 us -> 82.1 us  [dp_swap(): return lax.ppermute(array, 'dp', flip_pairs(lax.axis_size('dp'), bit))]
    dot_general x12 -> x24, matrix products: 23.8 us -> 55.8 us  [dot(): return jnp.dot(left, right, preferred_element_type=wide_type)]
    unnamed x160 -> x253, local copies, waits for them, and re-layouts: 6.54 us -> 29.5 us
    ppermute x48 -> x33, starting transfers between devices: 47 us -> 26.5 us  [dp_swap(): return lax.ppermute(array, 'dp', flip_pairs(lax.axis_size('dp'), bit))]
    dot_general x8 -> x16, matrix products: 22.5 us -> 42 us  [dot_tn(): lax.dot_general(left, right, (((0,), (0,)), ((), ())), preferred_element_...]
    another operation x2 -> x13, local copies, waits for them, and re-layouts: 0.1 us -> 14.2 us  [the longest x11 12.2 us: on_device(): jnp.stack([member for args in layer_args for member in (args[0], args[1],...]
    dot_general x12 -> x16, matrix products: 44.7 us -> 31.9 us  [dot_nt(): lax.dot_general(left, right, (((1,), (1,)), ((), ())), preferred_element_...]
  transfers between devices with their start and end apart: 63 -> 49, of which waited for: 26 -> 20; matrix products, arithmetic and copies ran while one was open for 18% -> 54% of each run, Pallas kernels for 0% -> 0%
where the time goes in v2:
time: 429 us; the launch traced here: 422 us
  matrix products  130 us (30%)
  waiting for transfers between devices  102 us (24%)
  local copies, waits for them, and re-layouts  67.8 us (16%)
  other arithmetic  63.9 us (15%)
  starting transfers between devices  42.2 us (10%)
  between operations  16.5 us (4%)
    ppermute x33, waiting for transfers between devices, dp_swap(): return lax.ppermute(array, 'dp', flip_pairs(lax.axis_size('dp'), bit))  82.1 us
    dot_general x24, matrix products, dot(): return jnp.dot(left, right, preferred_element_type=wide_type)  55.8 us
    dot_general x16, matrix products, dot_tn(): lax.dot_general(left, right, (((0,), (0,)), ((), ())), preferred_element_...  42 us
    dot_general x16, matrix products, dot_nt(): lax.dot_general(left, right, (((1,), (1,)), ((), ())), preferred_element_...  31.9 us
    unnamed x253, local copies, waits for them, and re-layouts  29.5 us
    ppermute x33, starting transfers between devices, dp_swap(): return lax.ppermute(array, 'dp', flip_pairs(lax.axis_size('dp'), bit))  26.5 us
    ppermute x13, waiting for transfers between devices, mp_swap(): return lax.ppermute(array, 'mp', [(0, 1), (1, 0)])  17.5 us
    ppermute x13, starting transfers between devices, mp_swap(): return lax.ppermute(array, 'mp', [(0, 1), (1, 0)])  15.4 us
  transfers between devices with their start and end apart: 49, of which 20 were waited for; matrix products, arithmetic and copies ran while one was open for 54% of the time, Pallas kernels for 0%

profile of v2, /device:TPU:0, one launch (start us, length us, event | category | flops | bytes accessed | tf_op | source)
XLA Modules:
  0.0 422.3 jit_solution(6354050077508389660)
XLA Ops:
  40.8 4.4 %convolution_convert_fusion.1.refs_0_ = bf16[512,1536]{1,0:T(8,128)(2,1)} fusion(bf16[768,1536]{1,0:T(8,128)(2,1)} %constant.375.clone, f32[512]{0:T(512)S(1)} %fusion.116, bf16[256,768]{1,0:T(8,128)(2,1)} %copy-done.41, bf16[256,768]{1,0:T(8,128)(2,1)S(1)} %get-tuple-element.73), kind=kOutput, calls=%fused_computation.2 | convolution fusion | flops 1211105280 | bytes 4720640 | tf_op jit(solution)/shard_map/dot_general | solution.py:24
  69.4 9.0 %collective-permute-done.3 = bf16[384,768]{1,0:T(8,128)(2,1)S(1)} collective-permute-done((bf16[384,768]{1,0:T(8,128)(2,1)}, bf16[384,768]{1,0:T(8,128)(2,1)S(1)}, u32[]{:S(2)}, u32[]{:S(2)}) %collective-permute-start.3) | collective-permute-done | bytes 589856 | tf_op jit(solution)/shard_map/ppermute | solution.py:85
  80.6 7.6 %collective-permute-done.7 = bf16[384,768]{1,0:T(8,128)(2,1)S(1)} collective-permute-done((bf16[384,768]{1,0:T(8,128)(2,1)S(1)}, bf16[384,768]{1,0:T(8,128)(2,1)S(1)}, u32[]{:S(2)}, u32[]{:S(2)}) %collective-permute-start.7) | collective-permute-done | bytes 589856 | tf_op jit(solution)/shard_map/ppermute | solution.py:85
  163.5 4.2 add_convert_fusion.9
  172.8 4.6 %multiply_reduce_fusion.1 = (f32[768]{0:T(1024)}, f32[512]{0:T(512)S(1)}, f32[512]{0:T(512)S(1)}, f32[768]{0:T(1024)}, f32[512,768]{1,0:T(8,128)S(1)}) fusion(f32[512,768]{1,0:T(8,128)S(1)} %copy-done.11, f32[512]{0:T(512)S(1)} %copy-done.62, f32[512]{0:T(512)S(1)} %copy-done.55, f32[768]{0:T(1024)S(1)} %copy-done.52, ...), kind=kOutput, calls=%fused_computation.42 | convolution fusion | flops 613807616 | bytes 9861120 | tf_op jit(solution)/shard_map/dot_general | solution.py:32
  179.0 4.4 %fusion.27 = f32[512,768]{1,0:T(8,128)} fusion(bf16[768,768]{1,0:T(8,128)(2,1)} %constant.380, bf16[512,1024]{1,0:T(8,128)(2,1)} %dynamic-slice_bitcast_fusion, f32[512,768]{1,0:T(8,128)} %subtract_multiply_fusion.2), kind=kOutput, calls=%fused_computation.151 | convolution fusion | flops 1007419392 | bytes 4849664 | tf_op jit(solution)/shard_map/dot_general | solution.py:24
  183.4 6.7 %multiply_reduce_fusion.2 = (f32[768]{0:T(1024)}, f32[512]{0:T(512)S(1)}, f32[512]{0:T(512)S(1)}, f32[768]{0:T(1024)}, f32[512,768]{1,0:T(8,128)}) fusion(f32[512,768]{1,0:T(8,128)} %copy-done.14, f32[512]{0:T(512)S(1)} %copy-done.82, f32[512]{0:T(512)S(1)} %copy-done.59, f32[768]{0:T(1024)S(1)} %copy-done.76, f32[512]{0:T(512)S(1)} %copy-done.67, ...), kind=kOutput, calls=%fused_computation.47 | convolution fusion | flops 1012528640 | bytes 9587712 | tf_op jit(solution)/shard_map/dot_general | solution.py:24
  190.2 4.3 %convert_reduce_fusion.9 = (f32[768]{0:T(1024)}, bf16[512,768]{1,0:T(8,128)(2,1)S(1)}, f32[512,768]{1,0:T(8,128)}) fusion(f32[512]{0:T(512)S(1)} %broadcast_multiply_fusion.2, f32[512,768]{1,0:T(8,128)} %copy-done.14, f32[512]{0:T(512)S(1)} %copy-done.59, f32[512]{0:T(512)S(1)} %broadcast_multiply_fusion.3, f32[512,768]{1,0:T(8,128)} %get-tuple-element.96, ...), kind=kLoop, calls=%fused_computation.48 | loop fusion | flops 3931392 | bytes 5519360 | tf_op jit(solution)/shard_map/reduce_sum | solution.py:213
  219.3 4.4 %add_convert_fusion.4.refs_0_ = bf16[768,768]{1,0:T(8,128)(2,1)} fusion(f32[768,768]{1,0:T(8,128)} %fusion.121, bf16[512,768]{1,0:T(8,128)(2,1)} %copy-done.100, f32[512,768]{1,0:T(8,128)} %copy-done.111), kind=kOutput, calls=%fused_computation.15 | convolution fusion | flops 608698368 | bytes 5898240 | tf_op jit(solution)/shard_map/dot_general | solution.py:28
  229.6 4.5 %add_convert_fusion.5 = bf16[768,768]{1,0:T(8,128)(2,1)} fusion(f32[768,768]{1,0:T(8,128)} %fusion.120, bf16[512,768]{1,0:T(8,128)(2,1)} %copy-done.100, f32[512,768]{1,0:T(8,128)} %copy-done.109), kind=kOutput, calls=%fused_computation.16 | convolution fusion | flops 608698368 | bytes 5898240 | tf_op jit(solution)/shard_map/dot_general | solution.py:28
  240.2 4.3 %collective-permute-done.43 = bf16[2,96,768]{2,1,0:T(8,128)(2,1)S(1)} collective-permute-done((bf16[2,96,768]{2,1,0:T(8,128)(2,1)S(1)}, bf16[2,96,768]{2,1,0:T(8,128)(2,1)S(1)}, u32[]{:S(2)}, u32[]{:S(2)}) %collective-permute-start.43) | collective-permute-done | bytes 294944 | tf_op jit(solution)/shard_map/ppermute | solution.py:85
  257.9 5.5 %multiply_reduce_fusion.3 = (f32[768]{0:T(1024)}, f32[512]{0:T(512)}, f32[512]{0:T(512)}, f32[768]{0:T(1024)}, f32[512,768]{1,0:T(8,128)}) fusion(f32[512,768]{1,0:T(8,128)} %copy-done.1, f32[512]{0:T(512)S(1)} %copy-done.47, f32[512]{0:T(512)S(1)} %broadcast_multiply_fusion.11, f32[768]{0:T(1024)S(1)} %get-tuple-element.43, ...), kind=kLoop, calls=%fused_computation.49 | loop fusion | flops 5109248 | bytes 8668160 | tf_op jit(solution)/shard_map/reduce_sum | solution.py:226
  285.0 6.2 %collective-permute-done.35 = bf16[2,2,96,768]{3,2,1,0:T(8,128)(2,1)S(1)} collective-permute-done((bf16[2,2,96,768]{3,2,1,0:T(8,128)(2,1)S(1)}, bf16[2,2,96,768]{3,2,1,0:T(8,128)(2,1)S(1)}, u32[]{:S(2)}, u32[]{:S(2)}) %collective-permute-start.35) | collective-permute-done | bytes 589856 | tf_op jit(solution)/shard_map/ppermute | solution.py:85
  292.3 9.1 %collective-permute-done.27 = bf16[768,768]{1,0:T(8,128)(2,1)S(1)} collective-permute-done((bf16[768,768]{1,0:T(8,128)(2,1)}, bf16[768,768]{1,0:T(8,128)(2,1)S(1)}, u32[]{:S(2)}, u32[]{:S(2)}) %collective-permute-start.27) | collective-permute-done | bytes 1179680 | tf_op jit(solution)/shard_map/ppermute | solution.py:89
  303.4 8.4 %collective-permute-done.36 = bf16[2,96,768]{2,1,0:T(8,128)(2,1)S(1)} collective-permute-done((bf16[2,96,768]{2,1,0:T(8,128)(2,1)S(1)}, bf16[2,96,768]{2,1,0:T(8,128)(2,1)S(1)}, u32[]{:S(2)}, u32[]{:S(2)}) %collective-permute-start.36) | collective-permute-done | bytes 294944 | tf_op jit(solution)/shard_map/ppermute | solution.py:85
  312.2 7.5 %collective-permute-done.28 = bf16[2,2,96,768]{3,2,0,1:T(8,128)(2,1)S(1)} collective-permute-done((bf16[2,2,96,768]{3,2,0,1:T(8,128)(2,1)S(1)}, bf16[2,2,96,768]{3,2,0,1:T(8,128)(2,1)S(1)}, u32[]{:S(2)}, u32[]{:S(2)}) %collective-permute-start.28) | collective-permute-done | bytes 589856 | tf_op jit(solution)/shard_map/ppermute | solution.py:85
  326.2 7.8 %collective-permute-done.29 = bf16[2,96,768]{2,1,0:T(8,128)(2,1)S(1)} collective-permute-done((bf16[2,96,768]{2,1,0:T(8,128)(2,1)S(1)}, bf16[2,96,768]{2,1,0:T(8,128)(2,1)S(1)}, u32[]{:S(2)}, u32[]{:S(2)}) %collective-permute-start.29) | collective-permute-done | bytes 294944 | tf_op jit(solution)/shard_map/ppermute | solution.py:85
  334.9 4.6 %fusion.28 = f32[512,768]{1,0:T(8,128)} fusion(bf16[768,768]{1,0:T(8,128)(2,1)} %constant.380, bf16[512,1024]{1,0:T(8,128)(2,1)} %dynamic-slice_bitcast_fusion, f32[512,768]{1,0:T(8,128)} %subtract_multiply_fusion), kind=kOutput, calls=%fused_computation.152 | convolution fusion | flops 1007419392 | bytes 4849664 | tf_op jit(solution)/shard_map/dot_general | solution.py:24
  345.5 8.9 %collective-permute-done.39 = bf16[2,96,768]{2,1,0:T(8,128)(2,1)S(1)} collective-permute-done((bf16[2,96,768]{2,1,0:T(8,128)(2,1)S(1)}, bf16[2,96,768]{2,1,0:T(8,128)(2,1)S(1)}, u32[]{:S(2)}, u32[]{:S(2)}) %collective-permute-start.39) | collective-permute-done | bytes 294944 | tf_op jit(solution)/shard_map/ppermute | solution.py:85
  356.0 5.1 %fusion.12 = bf16[512,768]{1,0:T(8,128)(2,1)} fusion(f32[512,768]{1,0:T(8,128)} %subtract_multiply_fusion, f32[512,768]{1,0:T(8,128)} %fusion.28, bf16[768,768]{1,0:T(8,128)(2,1)} %constant.381, f32[512]{0:T(512)S(1)} %copy-done.67, bf16[512,1024]{1,0:T(8,128)(2,1)} %dynamic-slice_bitcast_fusion), kind=kOutput, calls=%fused_computation.32 | convolution fusion | flops 1008992256 | bytes 7211008 | tf_op jit(solution)/shard_map/dot_general | solution.py:24
  367.8 4.0 collective-permute-done.40
  374.7 7.5 %collective-permute-done.33 = bf16[2,2,96,768]{3,2,0,1:T(8,128)(2,1)S(1)} collective-permute-done((bf16[2,2,96,768]{3,2,0,1:T(8,128)(2,1)S(1)}, bf16[2,2,96,768]{3,2,0,1:T(8,128)(2,1)S(1)}, u32[]{:S(2)}, u32[]{:S(2)}) %collective-permute-start.33) | collective-permute-done | bytes 589856 | tf_op jit(solution)/shard_map/ppermute | solution.py:85
  387.9 7.6 %collective-permute-done.25 = f32[13824]{0:T(1024)S(1)} collective-permute-done((f32[13824]{0:T(1024)S(1)}, f32[13824]{0:T(1024)S(1)}, u32[]{:S(2)}, u32[]{:S(2)}) %collective-permute-start.25) | collective-permute-done | bytes 55328 | tf_op jit(solution)/shard_map/ppermute | solution.py:89
  409.4 3.6 copy.68
  (520 shorter events, 261.9 us)
Async XLA Ops:
  7.2 110.0 %all-gather.5.cloned.1.call-start = ((), (), s32[]{:S(2)}) async-start(), calls=%async_computation.2 | async-start | bytes 2654208 | tf_op jit(solution)/shard_map/all_gather | solution.py:452
  9.4 28.5 %collective-permute-start.1 = (bf16[192,768]{1,0:T(8,128)(2,1)}, bf16[192,768]{1,0:T(8,128)(2,1)}, u32[]{:S(2)}, u32[]{:S(2)}) collective-permute-start(bf16[192,768]{1,0:T(8,128)(2,1)} %dynamic_slice.138), channel_id=1, source_target_pairs={{0,1},{1,0},{2,3},{3,2},{4,5},{5,4},{6,7},{7,6},{8,9},{9,8},{10,11... | collective-permute-start | bytes 884744 | tf_op jit(solution)/shard_map/ppermute | solution.py:89
  13.5 26.0 %collective-permute-start = (bf16[256,768]{1,0:T(8,128)(2,1)S(1)}, bf16[256,768]{1,0:T(8,128)(2,1)S(1)}, u32[]{:S(2)}, u32[]{:S(2)}) collective-permute-start(bf16[256,768]{1,0:T(8,128)(2,1)S(1)} %get-tuple-element.74), channel_id=1, source_target_pairs={{0,1},{1,0},{2,3},{3,2},{4,5},{5,4},{6,7},{7,6},{8,9},{9,8},{10,11... | collective-permute-start | bytes 1179656 | tf_op jit(solution)/shard_map/ppermute | solution.py:89
  16.3 40.7 %collective-permute-start.10 = (bf16[192,768]{1,0:T(8,128)(2,1)}, bf16[192,768]{1,0:T(8,128)(2,1)}, u32[]{:S(2)}, u32[]{:S(2)}) collective-permute-start(bf16[192,768]{1,0:T(8,128)(2,1)} %pad_maximum_fusion.4), channel_id=1, source_target_pairs={{0,1},{1,0},{2,3},{3,2},{4,5},{5,4},{6,7},{7,6},{8,9},{9,8},{10,11... | collective-permute-start | bytes 884744 | tf_op jit(solution)/shard_map/ppermute | solution.py:89
  57.0 199.2 %reduce-scatter.2.cloned.1.call-start = ((), (), s32[]{:S(2)}) async-start(), calls=%async_computation.1 | async-start | bytes 2654208 | tf_op jit(solution)/shard_map/reduce_scatter | solution.py:332
  57.3 21.1 %collective-permute-start.3 = (bf16[384,768]{1,0:T(8,128)(2,1)}, bf16[384,768]{1,0:T(8,128)(2,1)S(1)}, u32[]{:S(2)}, u32[]{:S(2)}) collective-permute-start(bf16[384,768]{1,0:T(8,128)(2,1)} %maximum_select_fusion.8.refs_1_), channel_id=1, source_target_pairs={{0,4},{2,6},{4,0},{6,2},{8,12},{10,14},{12,8},{14,10},{16,20},{18,... | collective-permute-start | bytes 1769480 | tf_op jit(solution)/shard_map/ppermute | solution.py:85
  64.7 23.5 %collective-permute-start.7 = (bf16[384,768]{1,0:T(8,128)(2,1)S(1)}, bf16[384,768]{1,0:T(8,128)(2,1)S(1)}, u32[]{:S(2)}, u32[]{:S(2)}) collective-permute-start(bf16[384,768]{1,0:T(8,128)(2,1)S(1)} %maximum_select_fusion.9), channel_id=1, source_target_pairs={{0,8},{2,10},{4,12},{6,14},{8,0},{10,2},{12,4},{14,6},{16,24},{18,... | collective-permute-start | bytes 1769480 | tf_op jit(solution)/shard_map/ppermute | solution.py:85
  106.8 23.4 %collective-permute-start.14 = (bf16[256,768]{1,0:T(8,128)(2,1)}, bf16[256,768]{1,0:T(8,128)(2,1)}, u32[]{:S(2)}, u32[]{:S(2)}) collective-permute-start(bf16[256,768]{1,0:T(8,128)(2,1)} %gate.10), channel_id=1, source_target_pairs={{0,1},{1,0},{2,3},{3,2},{4,5},{5,4},{6,7},{7,6},{8,9},{9,8},{10,11... | collective-permute-start | bytes 1179656 | tf_op jit(solution)/shard_map/ppermute | solution.py:89
  145.7 240.1 %collective-permute-start.13 = (bf16[1,256,768]{2,1,0:T(8,128)(2,1)}, bf16[1,256,768]{2,1,0:T(8,128)(2,1)}, u32[]{:S(2)}, u32[]{:S(2)}) collective-permute-start(bf16[1,256,768]{2,1,0:T(8,128)(2,1)} %get-tuple-element.72), channel_id=1, source_target_pairs={{0,1},{1,0},{2,3},{3,2},{4,5},{5,4},{6,7},{7,6},{8,9},{9,8},{10,11... | collective-permute-start | bytes 1179656 | tf_op jit(solution)/shard_map/ppermute | solution.py:89
  163.3 240.4 %all-gather.7.cloned.1.call-start = ((), (), s32[]{:S(2)}) async-start(), calls=%async_computation.3 | async-start | bytes 5013504 | tf_op jit(solution)/shard_map/all_gather | solution.py:361
  167.7 43.0 %collective-permute-start.18 = (bf16[768,768]{1,0:T(8,128)(2,1)}, bf16[768,768]{1,0:T(8,128)(2,1)}, u32[]{:S(2)}, u32[]{:S(2)}) collective-permute-start(bf16[768,768]{1,0:T(8,128)(2,1)} %add_convert_fusion.9), channel_id=1, source_target_pairs={{0,1},{1,0},{2,3},{3,2},{4,5},{5,4},{6,7},{7,6},{8,9},{9,8},{10,11... | collective-permute-start | bytes 3538952 | tf_op jit(solution)/shard_map/ppermute | solution.py:89
  195.8 18.0 %collective-permute-start.17 = (bf16[512,768]{1,0:T(8,128)(2,1)S(1)}, bf16[512,768]{1,0:T(8,128)(2,1)S(1)}, u32[]{:S(2)}, u32[]{:S(2)}) collective-permute-start(bf16[512,768]{1,0:T(8,128)(2,1)S(1)} %get-tuple-element.51), channel_id=1, source_target_pairs={{0,2},{2,0},{4,6},{6,4},{8,10},{10,8},{12,14},{14,12},{16,18},{18,... | collective-permute-start | bytes 2359304 | tf_op jit(solution)/shard_map/ppermute | solution.py:85
  213.4 20.7 %collective-permute-start.42 = (bf16[2,2,96,768]{3,2,1,0:T(8,128)(2,1)}, bf16[2,2,96,768]{3,2,1,0:T(8,128)(2,1)}, u32[]{:S(2)}, u32[]{:S(2)}) collective-permute-start(bf16[2,2,96,768]{3,2,1,0:T(8,128)(2,1)} %dynamic-slice_bitcast_fusion.3), channel_id=1, source_target_pairs={{0,4},{2,6},{4,0},{6,2},{8,12},{10,14},{12,8},{14,10},{16,20},{18,... | collective-permute-start | bytes 1769480 | tf_op jit(solution)/shard_map/ppermute | solution.py:85
  227.9 30.0 %collective-permute-start.19 = (bf16[512,768]{1,0:T(8,128)(2,1)}, bf16[512,768]{1,0:T(8,128)(2,1)}, u32[]{:S(2)}, u32[]{:S(2)}) collective-permute-start(bf16[512,768]{1,0:T(8,128)(2,1)} %gate.11), channel_id=1, source_target_pairs={{0,2},{2,0},{4,6},{6,4},{8,10},{10,8},{12,14},{14,12},{16,18},{18,... | collective-permute-start | bytes 2359304 | tf_op jit(solution)/shard_map/ppermute | solution.py:85
  228.1 44.0 %collective-permute-start.26 = (bf16[768,768]{1,0:T(8,128)(2,1)}, bf16[768,768]{1,0:T(8,128)(2,1)S(1)}, u32[]{:S(2)}, u32[]{:S(2)}) collective-permute-start(bf16[768,768]{1,0:T(8,128)(2,1)} %gate.12), channel_id=1, source_target_pairs={{0,1},{1,0},{2,3},{3,2},{4,5},{5,4},{6,7},{7,6},{8,9},{9,8},{10,11... | collective-permute-start | bytes 3538952 | tf_op jit(solution)/shard_map/ppermute | solution.py:89
  274.7 26.7 %collective-permute-start.27 = (bf16[768,768]{1,0:T(8,128)(2,1)}, bf16[768,768]{1,0:T(8,128)(2,1)S(1)}, u32[]{:S(2)}, u32[]{:S(2)}) collective-permute-start(bf16[768,768]{1,0:T(8,128)(2,1)} %gate.13), channel_id=1, source_target_pairs={{0,1},{1,0},{2,3},{3,2},{4,5},{5,4},{6,7},{7,6},{8,9},{9,8},{10,11... | collective-permute-start | bytes 3538952 | tf_op jit(solution)/shard_map/ppermute | solution.py:89
  291.3 20.5 %collective-permute-start.36 = (bf16[2,96,768]{2,1,0:T(8,128)(2,1)S(1)}, bf16[2,96,768]{2,1,0:T(8,128)(2,1)S(1)}, u32[]{:S(2)}, u32[]{:S(2)}) collective-permute-start(bf16[2,96,768]{2,1,0:T(8,128)(2,1)S(1)} %dynamic-slice_bitcast_fusion.10), channel_id=1, source_target_pairs={{0,8},{2,10},{4,12},{6,14},{8,0},{10,2},{12,4},{14,6},{16,24},{18,... | collective-permute-start | bytes 884744 | tf_op jit(solution)/shard_map/ppermute | solution.py:85
  301.9 17.8 %collective-permute-start.28 = (bf16[2,2,96,768]{3,2,0,1:T(8,128)(2,1)S(1)}, bf16[2,2,96,768]{3,2,0,1:T(8,128)(2,1)S(1)}, u32[]{:S(2)}, u32[]{:S(2)}) collective-permute-start(bf16[2,2,96,768]{3,2,0,1:T(8,128)(2,1)S(1)} %bitcast.239), channel_id=1, source_target_pairs={{0,4},{2,6},{4,0},{6,2},{8,12},{10,14},{12,8},{14,10},{16,20},{18,... | collective-permute-start | bytes 1769480 | tf_op jit(solution)/shard_map/ppermute | solution.py:85
  303.3 19.7 %collective-permute-start.21 = (f32[13824]{0:T(1024)S(1)}, f32[13824]{0:T(1024)S(1)}, u32[]{:S(2)}, u32[]{:S(2)}) collective-permute-start(f32[13824]{0:T(1024)S(1)} %constant_dynamic-update-slice_fusion), channel_id=1, source_target_pairs={{0,2},{2,0},{4,6},{6,4},{8,10},{10,8},{12,14},{14,12},{16,18},{18,... | collective-permute-start | bytes 165896 | tf_op jit(solution)/shard_map/ppermute | solution.py:85
  325.1 16.9 %collective-permute-start.38 = (bf16[96,768]{1,0:T(8,128)(2,1)S(1)}, bf16[96,768]{1,0:T(8,128)(2,1)S(1)}, u32[]{:S(2)}, u32[]{:S(2)}) collective-permute-start(bf16[96,768]{1,0:T(8,128)(2,1)S(1)} %fusion.88), channel_id=1, source_target_pairs={{0,16},{2,18},{4,20},{6,22},{8,24},{10,26},{12,28},{14,30},{16,0},... | collective-permute-start | bytes 442376 | tf_op jit(solution)/shard_map/ppermute | solution.py:85
  339.5 21.6 %collective-permute-start.23 = (f32[13824]{0:T(1024)S(1)}, f32[13824]{0:T(1024)S(1)}, u32[]{:S(2)}, u32[]{:S(2)}) collective-permute-start(f32[13824]{0:T(1024)S(1)} %add.744), channel_id=1, source_target_pairs={{0,8},{2,10},{4,12},{6,14},{8,0},{10,2},{12,4},{14,6},{16,24},{18,... | collective-permute-start | bytes 165896 | tf_op jit(solution)/shard_map/ppermute | solution.py:85
  361.1 24.1 %collective-permute-start.24 = (f32[13824]{0:T(1024)S(1)}, f32[13824]{0:T(1024)S(1)}, u32[]{:S(2)}, u32[]{:S(2)}) collective-permute-start(f32[13824]{0:T(1024)S(1)} %add.745), channel_id=1, source_target_pairs={{0,16},{2,18},{4,20},{6,22},{8,24},{10,26},{12,28},{14,30},{16,0},... | collective-permute-start | bytes 165896 | tf_op jit(solution)/shard_map/ppermute | solution.py:85
  373.4 24.7 %collective-permute-start.41 = (bf16[768,768]{1,0:T(8,128)(2,1)S(1)}, bf16[768,768]{1,0:T(8,128)(2,1)S(1)}, u32[]{:S(2)}, u32[]{:S(2)}) collective-permute-start(bf16[768,768]{1,0:T(8,128)(2,1)S(1)} %bitcast.205), channel_id=1, source_target_pairs={{0,2},{2,0},{4,6},{6,4},{8,10},{10,8},{12,14},{14,12},{16,18},{18,... | collective-permute-start | bytes 3538952 | tf_op jit(solution)/shard_map/ppermute | solution.py:85
  382.5 18.3 %collective-permute-start.34 = (bf16[768,768]{1,0:T(8,128)(2,1)S(1)}, bf16[768,768]{1,0:T(8,128)(2,1)S(1)}, u32[]{:S(2)}, u32[]{:S(2)}) collective-permute-start(bf16[768,768]{1,0:T(8,128)(2,1)S(1)} %bitcast.207), channel_id=1, source_target_pairs={{0,2},{2,0},{4,6},{6,4},{8,10},{10,8},{12,14},{14,12},{16,18},{18,... | collective-permute-start | bytes 3538952 | tf_op jit(solution)/shard_map/ppermute | solution.py:85
  (145 other events, 995.2 us)
Sparse Core Ops, SparseCore 0:
  57.2 60.0 all-gather.4
  163.5 69.6 reduce-scatter.1
  264.4 62.5 all-gather.6
